TPU v7x, 32 devices: a whole 2x2x4 slice. The times are simulated.
32 devices in a mesh: ctx: 16 (over z, y, x), head: 2 (over core).
Axes of the slice: x: 2, y: 2, z: 4, core: 2. Of those that a mesh axis runs over, the one named last changes fastest.
Arguments:
- query_in: float32 [16384, 16, 128], P('ctx', 'head'), may hold values from -6 to 6
- key_in: float32 [16384, 16, 128], P('ctx', 'head'), may hold values from -6 to 6
- value_in: float32 [16384, 32, 128], P('ctx', 'head'), may hold values from -6 to 6
- gate_in: float32 [16384, 32, 128], P('ctx', 'head'), may hold values from -6 to 6
- log_gate: float32 [32, 16384], P('head', 'ctx'), may hold values from -1 to 0, as said below
- strength: float32 [32, 16384], P('head', 'ctx'), may hold values from 0.005 to 0.05
- query_conv: float32 [4, 16, 128], P(None, 'head'), may hold values from -3 to 3
- key_conv: float32 [4, 16, 128], P(None, 'head'), may hold values from -3 to 3
- value_conv: float32 [4, 32, 128], P(None, 'head'), may hold values from -3 to 3
- norm_gain: float32 [128], replicated, may hold values from 0.1 to 1.9
- out_weight: bfloat16 [4096, 2048], P('head'), may hold values from -0.09375 to 0.09375
Outputs:
- mixed: float32 [16384, 2048], P(('ctx', 'head'))
Inputs may be any that keep to these rules, and one draw needn't show every extreme that they name: `log_gate`: the logarithm of head h's decay factor at a token.
All inputs are finite; a program needn't handle non-finite values.
Results may differ from a plain program's by a relative error of at most 0.015.
Values may be sent and summed in bfloat16 or wider, within the bound.
A program may use at most 192 MiB of HBM per device.

v0:
```python
import jax
import jax.numpy as jnp
from jax import lax
from jax.sharding import PartitionSpec as P

SPAN = 64


exact_precision = lax.Precision.HIGHEST
norm_epsilon = 1e-06


def from_behind(value, axis, steps):
    count = lax.axis_size(axis)
    initial, last = (max(0, -steps), min(count, count - steps))
    return lax.ppermute(value, axis, [(source, source + steps) for source in range(initial, last)])


def causal_mix(current, previous, kernel):
    kernel_width = kernel.shape[0]
    token_count = current.shape[0]
    padded = jnp.concatenate([previous, current], axis=0)
    summed = jnp.zeros(current.shape, jnp.float32)
    for offset in range(kernel_width):
        summed = summed + kernel[offset] * padded[offset : offset + token_count]
    return jax.nn.silu(summed)


def unit_rows(matrix):
    return matrix * lax.rsqrt(jnp.sum(matrix * matrix, axis=-1, keepdims=True) + norm_epsilon)


def to_blocks(matrix, block_size):
    token_count, head_count, width_count = matrix.shape
    return matrix.reshape(token_count // block_size, block_size, head_count, width_count).transpose(
        0, 2, 1, 3
    )


def gate_blocks(matrix, block_size):
    head_count, token_count = matrix.shape
    return matrix.reshape(head_count, token_count // block_size, block_size).transpose(1, 0, 2)


def prepare(
    query_in,
    key_in,
    value_in,
    query_prev,
    key_prev,
    value_prev,
    query_conv,
    key_conv,
    value_conv,
    block_size,
):
    group_ratio = value_in.shape[1] // query_in.shape[1]
    queries = unit_rows(causal_mix(query_in, query_prev, query_conv)) * query_in.shape[2] ** (-0.5)
    key_rows = unit_rows(causal_mix(key_in, key_prev, key_conv))
    values = causal_mix(value_in, value_prev, value_conv)
    queries = jnp.repeat(queries, group_ratio, axis=1)
    key_rows = jnp.repeat(key_rows, group_ratio, axis=1)
    return (
        to_blocks(queries, block_size),
        to_blocks(key_rows, block_size),
        to_blocks(values, block_size),
    )


def unit_inverse(mixing):
    block_size = mixing.shape[-1]
    identity_map = jnp.eye(block_size, dtype=jnp.float32)
    powered = -mixing
    inverse = identity_map + powered
    reach = 2
    while reach < block_size:
        powered = jnp.einsum("nhij,nhjk->nhik", powered, powered, precision=exact_precision)
        inverse = jnp.einsum(
            "nhij,nhjk->nhik", inverse, identity_map + powered, precision=exact_precision
        )
        reach = reach * 2
    return inverse


def span_setup(queries, key_rows, values, log_gate, strength):
    cumulative = jnp.cumsum(log_gate, axis=-1)
    block_size = cumulative.shape[-1]
    row_index = lax.broadcasted_iota(jnp.int32, (block_size, block_size), 0)
    col_index = lax.broadcasted_iota(jnp.int32, (block_size, block_size), 1)
    lower_mask = row_index >= col_index
    strict_mask = row_index > col_index
    differences = cumulative[..., :, None] - cumulative[..., None, :]
    decay_table = jnp.exp(jnp.where(lower_mask, differences, -jnp.inf))
    key_inner = jnp.einsum("nhcd,nhmd->nhcm", key_rows, key_rows, precision=exact_precision)
    mixing = jnp.where(strict_mask, strength[..., :, None] * key_inner * decay_table, 0.0)
    scores = jnp.where(
        lower_mask,
        jnp.einsum("nhcd,nhmd->nhcm", queries, key_rows, precision=exact_precision) * decay_table,
        0.0,
    )
    inverse = unit_inverse(mixing)
    fresh_values = jnp.einsum(
        "nhcm,nhmw->nhcw", inverse, strength[..., None] * values, precision=exact_precision
    )
    solved_keys = jnp.einsum(
        "nhcm,nhmd->nhcd",
        inverse,
        (strength * jnp.exp(cumulative))[..., None] * key_rows,
        precision=exact_precision,
    )
    lifted = jnp.exp(cumulative)[..., None] * queries
    carried = jnp.exp(cumulative[..., -1:] - cumulative)[..., None] * key_rows
    ending = jnp.exp(cumulative[..., -1])
    return (fresh_values, solved_keys, scores, lifted, carried, ending)


def run_spans(start_state, setup):

    def advance(carry_state, per_span):
        fresh_block, solved_block, score_block, lifted_block, carried_block, ending_block = per_span
        update = fresh_block - jnp.einsum(
            "hcd,hdw->hcw", solved_block, carry_state, precision=exact_precision
        )
        new_state = ending_block[:, None, None] * carry_state + jnp.einsum(
            "hcd,hcw->hdw", carried_block, update, precision=exact_precision
        )
        result = jnp.einsum("hcd,hdw->hcw", lifted_block, carry_state, precision=exact_precision)
        result = result + jnp.einsum("hcm,hmw->hcw", score_block, update, precision=exact_precision)
        return (new_state, result)

    return lax.scan(advance, start_state, setup)


def gated_norm(recurrent, gate_in, norm_gain):
    scaled = recurrent * lax.rsqrt(
        jnp.mean(recurrent * recurrent, axis=-1, keepdims=True) + norm_epsilon
    )
    return scaled * norm_gain * jax.nn.silu(gate_in)


def batched(left, right):
    return jnp.einsum("hij,hjk->hik", left, right, precision=exact_precision)


def on_device(
    query_in,
    key_in,
    value_in,
    gate_in,
    log_gate,
    strength,
    query_conv,
    key_conv,
    value_conv,
    norm_gain,
    out_weight,
):
    rim_count = query_conv.shape[0] - 1
    query_prev, key_prev, value_prev = from_behind(
        (query_in[-rim_count:], key_in[-rim_count:], value_in[-rim_count:]), "ctx", 1
    )
    queries, key_rows, values = prepare(
        query_in,
        key_in,
        value_in,
        query_prev,
        key_prev,
        value_prev,
        query_conv,
        key_conv,
        value_conv,
        SPAN,
    )
    setup = span_setup(
        queries, key_rows, values, gate_blocks(log_gate, SPAN), gate_blocks(strength, SPAN)
    )
    fresh_values, solved_keys, scores, lifted, carried, ending = setup
    token_count = query_in.shape[0]
    head_dev = values.shape[1]
    key_width = key_rows.shape[3]
    value_width = values.shape[3]
    identity_map = jnp.broadcast_to(
        jnp.eye(key_width, dtype=jnp.float32), (head_dev, key_width, key_width)
    )
    empty_state = jnp.zeros((head_dev, key_width, value_width), jnp.float32)
    start_state = jnp.concatenate([identity_map, empty_state], axis=2)
    widened = jnp.concatenate([jnp.zeros(key_rows.shape, jnp.float32), fresh_values], axis=3)
    widened_setup = (widened, solved_keys, scores, lifted, carried, ending)
    final_state, widened_out = run_spans(start_state, widened_setup)
    transition = final_state[:, :, :key_width]
    offset = final_state[:, :, key_width:]
    chain_count = lax.axis_size("ctx") - 1

    def chain_turn(turn_index, chain_carry):
        received = from_behind(chain_carry[1].astype(jnp.bfloat16), "ctx", 1).astype(jnp.float32)
        return (received, batched(transition, received) + offset)

    entering = lax.fori_loop(0, chain_count, chain_turn, (empty_state, offset))[0]
    recurrent = widened_out[..., key_width:] + jnp.einsum(
        "nhcd,hdw->nhcw", widened_out[..., :key_width], entering, precision=exact_precision
    )
    recurrent = recurrent.transpose(0, 2, 1, 3).reshape(token_count, head_dev, value_width)
    normed = (
        gated_norm(recurrent, gate_in, norm_gain)
        .astype(jnp.bfloat16)
        .reshape(token_count, head_dev * value_width)
    )
    return lax.psum_scatter(
        jnp.dot(normed, out_weight, preferred_element_type=jnp.float32).astype(jnp.bfloat16),
        "head",
        scatter_dimension=0,
        tiled=True,
    ).astype(jnp.float32)


def solution(mesh):
    in_specs = (
        P("ctx", "head", None),
        P("ctx", "head", None),
        P("ctx", "head", None),
        P("ctx", "head", None),
        P("head", "ctx"),
        P("head", "ctx"),
        P(None, "head", None),
        P(None, "head", None),
        P(None, "head", None),
        P(),
        P("head", None),
    )
    out_specs = P(("ctx", "head"), None)
    return jax.shard_map(
        on_device, mesh=mesh, in_specs=in_specs, out_specs=out_specs, check_vma=False
    )
```

profile of v0, /device:TPU:31, one launch (start us, length us, event | category | flops | bytes accessed | tf_op | source)
XLA Modules:
  0.0 831.7 jit_solution(2949192540368358925)
XLA Ops:
  15.2 3.5 reduce_window_sum.11
  32.4 15.4 %fusion.43 = f32[16,16,64,64]{3,2,1,0:T(8,128)} fusion(f32[16,16,64,128]{3,2,0,1:T(8,128)S(1)} %bitcast.137), kind=kOutput, calls=%fused_computation.59 | convolution fusion | flops 1610612736 | bytes 12582912 | tf_op jit(solution)/shard_map/nhcd,nhmd->nhcm/dot_general | solution.py:94
  47.9 18.7 %fusion.45 = f32[16,16,64,64]{3,2,1,0:T(8,128)S(1)} fusion(f32[16,16,64,64]{3,2,1,0:T(8,128)} %fusion.43, f32[16,16,64]{2,1,0:T(8,128)S(1)} %reduce_window_sum.11, f32[16,16,64]{2,1,0:T(8,128)S(1)} %bitcast.148, pred[64,64]{1,0:T(8,128)(4,1)S(1)} %get-tuple-element.154, pred[64,64]{1,0:T(8,128)(4,1)S(1)} %get-tuple-element.155), kind=kOutput, calls=%fused_computation.61 | convolution fusion | flops 811597824 | bytes 8527872 | tf_op jit(solution)/shard_map/nhij,nhjk->nhik/dot_general | solution.py:77
  66.5 11.4 %fusion.94 = f32[16,16,64,64]{3,2,1,0:T(8,128)S(1)} fusion(f32[16,16,64,64]{3,2,1,0:T(8,128)S(1)} %fusion.45), kind=kOutput, calls=%fused_computation.146 | convolution fusion | flops 805306368 | bytes 8388608 | tf_op jit(solution)/shard_map/nhij,nhjk->nhik/dot_general | solution.py:77
  78.0 24.4 %fusion.39 = f32[16,16,64,64]{3,2,1,0:T(8,128)} fusion(f32[16,16,64,64]{3,2,1,0:T(8,128)S(1)} %fusion.45, f32[16,16,64,64]{3,2,1,0:T(8,128)} %fusion.43, f32[16,16,64]{2,1,0:T(8,128)S(1)} %reduce_window_sum.11, f32[16,16,64]{2,1,0:T(8,128)S(1)} %bitcast.149, f32[64,64]{1,0:T(8,128)S(1)} %fusion.86, pred[64,64]{1,0:T(8,128)(4,1)S(1)} %get-tuple-element.154, ...), kind=kOutput, calls=%fused_computation.53 | convolution fusion | flops 813694976 | bytes 12738560 | tf_op jit(solution)/shard_map/nhij,nhjk->nhik/dot_general | solution.py:78
  102.4 11.4 %fusion.95 = f32[16,16,64,64]{3,2,1,0:T(8,128)S(1)} fusion(f32[16,16,64,64]{3,2,1,0:T(8,128)S(1)} %fusion.94), kind=kOutput, calls=%fused_computation.147 | convolution fusion | flops 805306368 | bytes 8388608 | tf_op jit(solution)/shard_map/nhij,nhjk->nhik/dot_general | solution.py:77
  113.8 12.4 %fusion.37 = f32[16,16,64,64]{3,2,1,0:T(8,128)} fusion(f32[16,16,64,64]{3,2,1,0:T(8,128)} %fusion.39, f32[16,16,64,64]{3,2,1,0:T(8,128)S(1)} %fusion.94, f32[64,64]{1,0:T(8,128)S(1)} %fusion.86), kind=kOutput, calls=%fused_computation.51 | convolution fusion | flops 806354944 | bytes 12599296 | tf_op jit(solution)/shard_map/nhij,nhjk->nhik/dot_general | solution.py:78
  126.3 11.4 %fusion.96 = f32[16,16,64,64]{3,2,1,0:T(8,128)S(1)} fusion(f32[16,16,64,64]{3,2,1,0:T(8,128)S(1)} %fusion.95), kind=kOutput, calls=%fused_computation.148 | convolution fusion | flops 805306368 | bytes 8388608 | tf_op jit(solution)/shard_map/nhij,nhjk->nhik/dot_general | solution.py:77
  137.7 12.2 %fusion.35 = f32[16,16,64,64]{3,2,1,0:T(8,128)} fusion(f32[16,16,64,64]{3,2,1,0:T(8,128)} %fusion.37, f32[16,16,64,64]{3,2,1,0:T(8,128)S(1)} %fusion.95, f32[64,64]{1,0:T(8,128)S(1)} %fusion.86), kind=kOutput, calls=%fused_computation.49 | convolution fusion | flops 806354944 | bytes 12599296 | tf_op jit(solution)/shard_map/nhij,nhjk->nhik/dot_general | solution.py:78
  149.9 12.0 %fusion.33 = f32[16,16,64,64]{3,2,1,0:T(8,128)} fusion(f32[16,16,64,64]{3,2,1,0:T(8,128)} %fusion.35, f32[16,16,64,64]{3,2,1,0:T(8,128)S(1)} %fusion.96, f32[64,64]{1,0:T(8,128)S(1)} %fusion.86), kind=kOutput, calls=%fused_computation.47 | convolution fusion | flops 806354944 | bytes 12599296 | tf_op jit(solution)/shard_map/nhij,nhjk->nhik/dot_general | solution.py:78
  161.8 11.3 %fusion.97 = f32[16,16,64,64]{3,2,1,0:T(8,128)} fusion(f32[16,16,64,64]{3,2,1,0:T(8,128)S(1)} %fusion.96), kind=kOutput, calls=%fused_computation.149 | convolution fusion | flops 805306368 | bytes 8388608 | tf_op jit(solution)/shard_map/nhij,nhjk->nhik/dot_general | solution.py:77
  180.4 3.7 copy-done.2
  184.4 16.1 %multiply_select_fusion = f32[16,16,64,64]{3,2,1,0:T(8,128)} fusion(f32[16,16,64]{2,1,0:T(8,128)S(1)} %reduce_window_sum.11, pred[64,64]{1,0:T(8,128)(4,1)S(1)} %get-tuple-element.154, f32[16,16,64,128]{3,2,0,1:T(8,128)S(1)} %bitcast.140, f32[16,16,64,128]{3,2,0,1:T(8,128)S(1)} %bitcast.142), kind=kOutput, calls=%fused_computation.43 | convolution fusion | flops 1614807040 | bytes 21041152 | tf_op jit(solution)/shard_map/nhcd,nhmd->nhcm/dot_general | solution.py:98
  200.4 11.5 %fusion.31 = f32[16,16,64,64]{3,2,1,0:T(8,128)S(1)} fusion(f32[16,16,64,64]{3,2,1,0:T(8,128)} %fusion.33, f32[16,16,64,64]{3,2,1,0:T(8,128)} %fusion.97, f32[64,64]{1,0:T(8,128)S(1)} %fusion.86), kind=kOutput, calls=%fused_computation.45 | convolution fusion | flops 806354944 | bytes 12599296 | tf_op jit(solution)/shard_map/nhij,nhjk->nhik/dot_general | solution.py:78
  211.9 6.6 broadcast_multiply_fusion.1
  218.5 12.4 %fusion.26 = f32[16,16,64,128]{3,2,1,0:T(8,128)} fusion(f32[16,16,64,64]{3,2,1,0:T(8,128)S(1)} %fusion.31, f32[16,16,64,128]{3,2,0,1:T(8,128)} %get-tuple-element.134), kind=kOutput, calls=%fused_computation.38 | convolution fusion | flops 1610612736 | bytes 20971520 | tf_op jit(solution)/shard_map/nhcm,nhmd->nhcd/dot_general | solution.py:105
  230.9 4.6 broadcast_multiply_fusion
  236.2 7.2 constant_dynamic-update-slice_fusion.2
  243.4 15.8 %divide_multiply_fusion = f32[1024,16,128]{2,1,0:T(8,128)} fusion(f32[1027,16,128]{2,1,0:T(8,128)} %constant_dynamic-update-slice_fusion.2, f32[1024,16,128]{2,1,0:T(8,128)} %param.17, f32[16,128]{1,0:T(8,128)S(1)} %get-tuple-element.142, f32[16,128]{1,0:T(8,128)S(1)} %get-tuple-element.143, f32[16,128]{1,0:T(8,128)S(1)} %get-tuple-element.141, ...), kind=kLoop, calls=%fused_computation.44 | loop fusion | flops 23068672 | bytes 41975808 | tf_op jit(solution)/shard_map/jit(silu)/mul | solution.py:26
  259.2 14.3 %fusion.20 = f32[16,16,64,128]{3,2,1,0:T(8,128)} fusion(f32[16,16,64,64]{3,2,1,0:T(8,128)S(1)} %fusion.31, f32[16,64,16,128]{3,2,1,0:T(8,128)} %bitcast.144, f32[16,16,64]{2,1,0:T(8,128)S(1)} %bitcast.150), kind=kOutput, calls=%fused_computation.31 | convolution fusion | flops 1612709888 | bytes 21037056 | tf_op jit(solution)/shard_map/nhcm,nhmw->nhcw/dot_general | solution.py:102
  273.5 11.4 %concatenate.18 = f32[16,16,64,256]{3,2,1,0:T(8,128)} pad(f32[16,16,64,128]{3,2,1,0:T(8,128)} %fusion.20, f32[]{:T(128)} %constant.30.clone.1), padding=0_0x0_0x0_0x128_0 | pad | bytes 25165828 | tf_op jit(solution)/shard_map/concatenate | solution.py:187
  284.9 198.1 %while.24 = (s32[]{:T(128)}, f32[16,128,256]{2,1,0:T(8,128)S(1)}, f32[16,16,64,256]{3,2,0,1:T(8,128)}, f32[16,16]{1,0:T(8,128)}, f32[16,16,64,128]{3,2,0,1:T(8,1...) while((s32[]{:T(128)}, f32[16,128,256]{2,1,0:T(8,128)S(1)}, ...), condition=%wide.region_4.5_spmd, body=%wide.region_3.4_spmd.sunk | while | flops 1410859008 | bytes 17829160 | solution.py:131
  293.9 3.5 multiply_add_fusion.2
  306.2 3.5 multiply_add_fusion.2
  318.6 3.5 multiply_add_fusion.2
  405.2 3.5 multiply_add_fusion.2
  479.4 3.5 multiply_add_fusion.2
  484.4 258.4 %while.25 = (s32[]{:T(128)}, f32[16,128,128]{2,1,0:T(8,128)}, bf16[16,128,128]{2,1,0:T(8,128)(2,1)}, f32[16,128,128]{2,1,0:T(8,128)}, f32[16,128,128]{2,1,0:T(8,128)S(1)}, /*index=5*/s32[]{:T(128)}) while((s32[]{:T(128)}, f32[16,128,128]{2,1,0:T(8,128)}, bf16[16,128,128]{2,1,0:T(8,128)(2,1)}, f32[16,128,128]{2,1,0:T(8,128)}, ...), condition=%wide.region_6.7_spmd, body=%wide.region_5.6_spmd.sunk | while | flops 403439616 | bytes 6815853 | solution.py:198
  485.7 15.5 %collective-permute-done = bf16[16,128,128]{2,1,0:T(8,128)(2,1)S(1)} collective-permute-done((bf16[16,128,128]{2,1,0:T(8,128)(2,1)}, bf16[16,128,128]{2,1,0:T(8,128)(2,1)S(1)}, u32[]{:S(2)}, u32[]{:S(2)}) %collective-permute-start) | collective-permute-done | bytes 524320 | tf_op jit(solution)/shard_map/while/body/eval_jaxpr/ppermute | solution.py:16
  506.2 13.2 %collective-permute-done = bf16[16,128,128]{2,1,0:T(8,128)(2,1)S(1)} collective-permute-done((bf16[16,128,128]{2,1,0:T(8,128)(2,1)}, bf16[16,128,128]{2,1,0:T(8,128)(2,1)S(1)}, u32[]{:S(2)}, u32[]{:S(2)}) %collective-permute-start) | collective-permute-done | bytes 524320 | tf_op jit(solution)/shard_map/while/body/eval_jaxpr/ppermute | solution.py:16
  524.5 12.3 %collective-permute-done = bf16[16,128,128]{2,1,0:T(8,128)(2,1)S(1)} collective-permute-done((bf16[16,128,128]{2,1,0:T(8,128)(2,1)}, bf16[16,128,128]{2,1,0:T(8,128)(2,1)S(1)}, u32[]{:S(2)}, u32[]{:S(2)}) %collective-permute-start) | collective-permute-done | bytes 524320 | tf_op jit(solution)/shard_map/while/body/eval_jaxpr/ppermute | solution.py:16
  541.9 11.4 %collective-permute-done = bf16[16,128,128]{2,1,0:T(8,128)(2,1)S(1)} collective-permute-done((bf16[16,128,128]{2,1,0:T(8,128)(2,1)}, bf16[16,128,128]{2,1,0:T(8,128)(2,1)S(1)}, u32[]{:S(2)}, u32[]{:S(2)}) %collective-permute-start) | collective-permute-done | bytes 524320 | tf_op jit(solution)/shard_map/while/body/eval_jaxpr/ppermute | solution.py:16
  558.4 10.5 %collective-permute-done = bf16[16,128,128]{2,1,0:T(8,128)(2,1)S(1)} collective-permute-done((bf16[16,128,128]{2,1,0:T(8,128)(2,1)}, bf16[16,128,128]{2,1,0:T(8,128)(2,1)S(1)}, u32[]{:S(2)}, u32[]{:S(2)}) %collective-permute-start) | collective-permute-done | bytes 524320 | tf_op jit(solution)/shard_map/while/body/eval_jaxpr/ppermute | solution.py:16
  573.9 9.5 %collective-permute-done = bf16[16,128,128]{2,1,0:T(8,128)(2,1)S(1)} collective-permute-done((bf16[16,128,128]{2,1,0:T(8,128)(2,1)}, bf16[16,128,128]{2,1,0:T(8,128)(2,1)S(1)}, u32[]{:S(2)}, u32[]{:S(2)}) %collective-permute-start) | collective-permute-done | bytes 524320 | tf_op jit(solution)/shard_map/while/body/eval_jaxpr/ppermute | solution.py:16
  588.4 9.9 %collective-permute-done = bf16[16,128,128]{2,1,0:T(8,128)(2,1)S(1)} collective-permute-done((bf16[16,128,128]{2,1,0:T(8,128)(2,1)}, bf16[16,128,128]{2,1,0:T(8,128)(2,1)S(1)}, u32[]{:S(2)}, u32[]{:S(2)}) %collective-permute-start) | collective-permute-done | bytes 524320 | tf_op jit(solution)/shard_map/while/body/eval_jaxpr/ppermute | solution.py:16
  603.4 10.2 %collective-permute-done = bf16[16,128,128]{2,1,0:T(8,128)(2,1)S(1)} collective-permute-done((bf16[16,128,128]{2,1,0:T(8,128)(2,1)}, bf16[16,128,128]{2,1,0:T(8,128)(2,1)S(1)}, u32[]{:S(2)}, u32[]{:S(2)}) %collective-permute-start) | collective-permute-done | bytes 524320 | tf_op jit(solution)/shard_map/while/body/eval_jaxpr/ppermute | solution.py:16
  618.6 10.6 %collective-permute-done = bf16[16,128,128]{2,1,0:T(8,128)(2,1)S(1)} collective-permute-done((bf16[16,128,128]{2,1,0:T(8,128)(2,1)}, bf16[16,128,128]{2,1,0:T(8,128)(2,1)S(1)}, u32[]{:S(2)}, u32[]{:S(2)}) %collective-permute-start) | collective-permute-done | bytes 524320 | tf_op jit(solution)/shard_map/while/body/eval_jaxpr/ppermute | solution.py:16
  634.3 10.6 %collective-permute-done = bf16[16,128,128]{2,1,0:T(8,128)(2,1)S(1)} collective-permute-done((bf16[16,128,128]{2,1,0:T(8,128)(2,1)}, bf16[16,128,128]{2,1,0:T(8,128)(2,1)S(1)}, u32[]{:S(2)}, u32[]{:S(2)}) %collective-permute-start) | collective-permute-done | bytes 524320 | tf_op jit(solution)/shard_map/while/body/eval_jaxpr/ppermute | solution.py:16
  650.0 11.1 %collective-permute-done = bf16[16,128,128]{2,1,0:T(8,128)(2,1)S(1)} collective-permute-done((bf16[16,128,128]{2,1,0:T(8,128)(2,1)}, bf16[16,128,128]{2,1,0:T(8,128)(2,1)S(1)}, u32[]{:S(2)}, u32[]{:S(2)}) %collective-permute-start) | collective-permute-done | bytes 524320 | tf_op jit(solution)/shard_map/while/body/eval_jaxpr/ppermute | solution.py:16
  666.1 12.5 %collective-permute-done = bf16[16,128,128]{2,1,0:T(8,128)(2,1)S(1)} collective-permute-done((bf16[16,128,128]{2,1,0:T(8,128)(2,1)}, bf16[16,128,128]{2,1,0:T(8,128)(2,1)S(1)}, u32[]{:S(2)}, u32[]{:S(2)}) %collective-permute-start) | collective-permute-done | bytes 524320 | tf_op jit(solution)/shard_map/while/body/eval_jaxpr/ppermute | solution.py:16
  683.7 13.8 %collective-permute-done = bf16[16,128,128]{2,1,0:T(8,128)(2,1)S(1)} collective-permute-done((bf16[16,128,128]{2,1,0:T(8,128)(2,1)}, bf16[16,128,128]{2,1,0:T(8,128)(2,1)S(1)}, u32[]{:S(2)}, u32[]{:S(2)}) %collective-permute-start) | collective-permute-done | bytes 524320 | tf_op jit(solution)/shard_map/while/body/eval_jaxpr/ppermute | solution.py:16
  702.6 15.2 %collective-permute-done = bf16[16,128,128]{2,1,0:T(8,128)(2,1)S(1)} collective-permute-done((bf16[16,128,128]{2,1,0:T(8,128)(2,1)}, bf16[16,128,128]{2,1,0:T(8,128)(2,1)S(1)}, u32[]{:S(2)}, u32[]{:S(2)}) %collective-permute-start) | collective-permute-done | bytes 524320 | tf_op jit(solution)/shard_map/while/body/eval_jaxpr/ppermute | solution.py:16
  722.8 16.2 %collective-permute-done = bf16[16,128,128]{2,1,0:T(8,128)(2,1)S(1)} collective-permute-done((bf16[16,128,128]{2,1,0:T(8,128)(2,1)}, bf16[16,128,128]{2,1,0:T(8,128)(2,1)S(1)}, u32[]{:S(2)}, u32[]{:S(2)}) %collective-permute-start) | collective-permute-done | bytes 524320 | tf_op jit(solution)/shard_map/while/body/eval_jaxpr/ppermute | solution.py:16
  742.8 15.2 %fusion.19 = (f32[16,64,16]{1,0,2:T(8,128)S(1)}, f32[16,16,64,128]{3,2,0,1:T(8,128)}) fusion(f32[16,16,64,256]{3,2,0,1:T(8,128)} %get-tuple-element.79, f32[16,128,128]{2,1,0:T(8,128)} %get-tuple-element.81), kind=kOutput, calls=%fused_computation.28 | convolution fusion | flops 3227500544 | bytes 26279936 | tf_op jit(solution)/shard_map/nhcd,hdw->nhcw/dot_general | solution.py:199
  758.3 11.0 %fusion.23 = bf16[1024,16,128]{2,1,0:T(8,128)(2,1)S(1)} fusion(f32[1024,16,128]{2,0,1:T(8,128)} %bitcast.145, f32[1024,16,128]{2,1,0:T(8,128)} %param.18, f32[128]{0:T(128)S(1)} %copy-done.6, f32[1024,16]{1,0:T(8,128)S(1)} %bitcast.147), kind=kLoop, calls=%fused_computation.35 | loop fusion | flops 16777216 | bytes 21037568 | tf_op jit(solution)/shard_map/convert_element_type | solution.py:205
  769.3 12.5 %fusion.75 = bf16[1024,2048]{1,0:T(8,128)(2,1)} fusion(bf16[2048,2048]{1,0:T(8,128)(2,1)} %param.25, bf16[128,8,16,128]{3,2,1,0:T(8,128)(2,1)S(1)} %bitcast.146), kind=kOutput, calls=%fused_computation.105 | convolution fusion | flops 8592031744 | bytes 16777216 | tf_op jit(solution)/shard_map/dot_general | solution.py:209
  781.9 38.6 %reduce-scatter.2.cloned.1.call-done = bf16[512,2048]{1,0:T(8,128)(2,1)} async-done(((bf16[1024,2048]{1,0:T(8,128)(2,1)}), bf16[512,2048]{1,0:T(8,128)(2,1)}) %reduce-scatter.2.cloned.1.call-update) | async-done | bytes 2097168 | tf_op jit(solution)/shard_map/reduce_scatter | solution.py:208
  820.5 4.1 convert_element_type.39
  (187 shorter events, 287.4 us)
Async XLA Ops:
  6.5 813.9 %reduce-scatter.2.cloned.1.call-start = ((), (), s32[]{:S(2)}) async-start(), calls=%async_computation.1 | async-start | bytes 6291456 | tf_op jit(solution)/shard_map/reduce_scatter | solution.py:208
  7.2 15.8 %collective-permute-start.1 = (f32[3,8,128]{2,1,0:T(8,128)S(1)}, f32[3,8,128]{2,1,0:T(8,128)S(1)}, u32[]{:S(2)}, u32[]{:S(2)}) collective-permute-start(f32[3,8,128]{2,1,0:T(8,128)S(1)} %slice.90), channel_id=1, source_target_pairs={{0,2},{2,4},{4,6},{6,8},{8,10},{10,12},{12,14},{14,16},{16,18},{18... | collective-permute-start | bytes 36872 | tf_op jit(solution)/shard_map/ppermute | solution.py:16
  9.3 226.3 %collective-permute-start.2 = (f32[3,16,128]{2,1,0:T(8,128)S(1)}, f32[3,16,128]{2,1,0:T(8,128)S(1)}, u32[]{:S(2)}, u32[]{:S(2)}) collective-permute-start(f32[3,16,128]{2,1,0:T(8,128)S(1)} %slice.98), channel_id=1, source_target_pairs={{0,2},{2,4},{4,6},{6,8},{8,10},{10,12},{12,14},{14,16},{16,18},{18... | collective-permute-start | bytes 73736 | tf_op jit(solution)/shard_map/ppermute | solution.py:16
  11.3 161.9 %collective-permute-start.3 = (f32[3,8,128]{2,1,0:T(8,128)S(1)}, f32[3,8,128]{2,1,0:T(8,128)S(1)}, u32[]{:S(2)}, u32[]{:S(2)}) collective-permute-start(f32[3,8,128]{2,1,0:T(8,128)S(1)} %slice.106), channel_id=1, source_target_pairs={{0,2},{2,4},{4,6},{6,8},{8,10},{10,12},{12,14},{14,16},{16,18},{18... | collective-permute-start | bytes 36872 | tf_op jit(solution)/shard_map/ppermute | solution.py:16
  21.4 4.5 copy-start.4
  32.4 15.4 %copy-start.1 = (f32[1024,8,2,128]{3,0,2,1:T(8,128)}, f32[1024,8,2,128]{3,0,2,1:T(8,128)S(1)}, u32[]{:S(2)}) copy-start(f32[1024,8,2,128]{3,0,2,1:T(8,128)S(1)} %broadcast_in_dim.58) | copy-start | bytes 25165828
  161.8 11.3 %copy-start.5 = (f32[1024,8,128]{2,1,0:T(8,128)S(1)}, f32[1024,8,128]{2,1,0:T(8,128)}, u32[]{:S(2)}) copy-start(f32[1024,8,128]{2,1,0:T(8,128)} %param.15) | copy-start | bytes 12582916
  178.7 5.4 slice-start
  179.6 4.8 slice-start.1
  180.4 3.7 copy-start.2
  218.5 12.5 %copy-start.3 = (f32[1024,8,2,128]{3,0,2,1:T(8,128)S(1)}, f32[1024,8,2,128]{3,0,2,1:T(8,128)}, u32[]{:S(2)}) copy-start(f32[1024,8,2,128]{3,0,2,1:T(8,128)} %copy-done.2) | copy-start | bytes 25165828
  273.5 11.4 %copy-start = (f32[16,128,256]{2,1,0:T(8,128)S(1)}, f32[16,128,256]{2,1,0:T(8,128)}, u32[]{:S(2)}) copy-start(f32[16,128,256]{2,1,0:T(8,128)} %concatenate.15) | copy-start | bytes 6291460
  484.4 16.7 %collective-permute-start = (bf16[16,128,128]{2,1,0:T(8,128)(2,1)}, bf16[16,128,128]{2,1,0:T(8,128)(2,1)S(1)}, u32[]{:S(2)}, u32[]{:S(2)}) collective-permute-start(bf16[16,128,128]{2,1,0:T(8,128)(2,1)} %get-tuple-element.278), channel_id=1, source_target_pairs={{0,2},{2,4},{4,6},{6,8},{8,10},{10,12},{12,14},{14,16},{16,18},{18... | collective-permute-start | bytes 1572872 | tf_op jit(solution)/shard_map/while/body/eval_jaxpr/ppermute | solution.py:16
  504.9 14.5 %collective-permute-start = (bf16[16,128,128]{2,1,0:T(8,128)(2,1)}, bf16[16,128,128]{2,1,0:T(8,128)(2,1)S(1)}, u32[]{:S(2)}, u32[]{:S(2)}) collective-permute-start(bf16[16,128,128]{2,1,0:T(8,128)(2,1)} %get-tuple-element.278), channel_id=1, source_target_pairs={{0,2},{2,4},{4,6},{6,8},{8,10},{10,12},{12,14},{14,16},{16,18},{18... | collective-permute-start | bytes 1572872 | tf_op jit(solution)/shard_map/while/body/eval_jaxpr/ppermute | solution.py:16
  523.2 13.6 %collective-permute-start = (bf16[16,128,128]{2,1,0:T(8,128)(2,1)}, bf16[16,128,128]{2,1,0:T(8,128)(2,1)S(1)}, u32[]{:S(2)}, u32[]{:S(2)}) collective-permute-start(bf16[16,128,128]{2,1,0:T(8,128)(2,1)} %get-tuple-element.278), channel_id=1, source_target_pairs={{0,2},{2,4},{4,6},{6,8},{8,10},{10,12},{12,14},{14,16},{16,18},{18... | collective-permute-start | bytes 1572872 | tf_op jit(solution)/shard_map/while/body/eval_jaxpr/ppermute | solution.py:16
  540.6 12.7 %collective-permute-start = (bf16[16,128,128]{2,1,0:T(8,128)(2,1)}, bf16[16,128,128]{2,1,0:T(8,128)(2,1)S(1)}, u32[]{:S(2)}, u32[]{:S(2)}) collective-permute-start(bf16[16,128,128]{2,1,0:T(8,128)(2,1)} %get-tuple-element.278), channel_id=1, source_target_pairs={{0,2},{2,4},{4,6},{6,8},{8,10},{10,12},{12,14},{14,16},{16,18},{18... | collective-permute-start | bytes 1572872 | tf_op jit(solution)/shard_map/while/body/eval_jaxpr/ppermute | solution.py:16
  557.1 11.8 %collective-permute-start = (bf16[16,128,128]{2,1,0:T(8,128)(2,1)}, bf16[16,128,128]{2,1,0:T(8,128)(2,1)S(1)}, u32[]{:S(2)}, u32[]{:S(2)}) collective-permute-start(bf16[16,128,128]{2,1,0:T(8,128)(2,1)} %get-tuple-element.278), channel_id=1, source_target_pairs={{0,2},{2,4},{4,6},{6,8},{8,10},{10,12},{12,14},{14,16},{16,18},{18... | collective-permute-start | bytes 1572872 | tf_op jit(solution)/shard_map/while/body/eval_jaxpr/ppermute | solution.py:16
  572.6 10.7 %collective-permute-start = (bf16[16,128,128]{2,1,0:T(8,128)(2,1)}, bf16[16,128,128]{2,1,0:T(8,128)(2,1)S(1)}, u32[]{:S(2)}, u32[]{:S(2)}) collective-permute-start(bf16[16,128,128]{2,1,0:T(8,128)(2,1)} %get-tuple-element.278), channel_id=1, source_target_pairs={{0,2},{2,4},{4,6},{6,8},{8,10},{10,12},{12,14},{14,16},{16,18},{18... | collective-permute-start | bytes 1572872 | tf_op jit(solution)/shard_map/while/body/eval_jaxpr/ppermute | solution.py:16
  587.1 11.2 %collective-permute-start = (bf16[16,128,128]{2,1,0:T(8,128)(2,1)}, bf16[16,128,128]{2,1,0:T(8,128)(2,1)S(1)}, u32[]{:S(2)}, u32[]{:S(2)}) collective-permute-start(bf16[16,128,128]{2,1,0:T(8,128)(2,1)} %get-tuple-element.278), channel_id=1, source_target_pairs={{0,2},{2,4},{4,6},{6,8},{8,10},{10,12},{12,14},{14,16},{16,18},{18... | collective-permute-start | bytes 1572872 | tf_op jit(solution)/shard_map/while/body/eval_jaxpr/ppermute | solution.py:16
  602.1 11.5 %collective-permute-start = (bf16[16,128,128]{2,1,0:T(8,128)(2,1)}, bf16[16,128,128]{2,1,0:T(8,128)(2,1)S(1)}, u32[]{:S(2)}, u32[]{:S(2)}) collective-permute-start(bf16[16,128,128]{2,1,0:T(8,128)(2,1)} %get-tuple-element.278), channel_id=1, source_target_pairs={{0,2},{2,4},{4,6},{6,8},{8,10},{10,12},{12,14},{14,16},{16,18},{18... | collective-permute-start | bytes 1572872 | tf_op jit(solution)/shard_map/while/body/eval_jaxpr/ppermute | solution.py:16
  617.3 11.9 %collective-permute-start = (bf16[16,128,128]{2,1,0:T(8,128)(2,1)}, bf16[16,128,128]{2,1,0:T(8,128)(2,1)S(1)}, u32[]{:S(2)}, u32[]{:S(2)}) collective-permute-start(bf16[16,128,128]{2,1,0:T(8,128)(2,1)} %get-tuple-element.278), channel_id=1, source_target_pairs={{0,2},{2,4},{4,6},{6,8},{8,10},{10,12},{12,14},{14,16},{16,18},{18... | collective-permute-start | bytes 1572872 | tf_op jit(solution)/shard_map/while/body/eval_jaxpr/ppermute | solution.py:16
  633.0 11.9 %collective-permute-start = (bf16[16,128,128]{2,1,0:T(8,128)(2,1)}, bf16[16,128,128]{2,1,0:T(8,128)(2,1)S(1)}, u32[]{:S(2)}, u32[]{:S(2)}) collective-permute-start(bf16[16,128,128]{2,1,0:T(8,128)(2,1)} %get-tuple-element.278), channel_id=1, source_target_pairs={{0,2},{2,4},{4,6},{6,8},{8,10},{10,12},{12,14},{14,16},{16,18},{18... | collective-permute-start | bytes 1572872 | tf_op jit(solution)/shard_map/while/body/eval_jaxpr/ppermute | solution.py:16
  648.7 12.4 %collective-permute-start = (bf16[16,128,128]{2,1,0:T(8,128)(2,1)}, bf16[16,128,128]{2,1,0:T(8,128)(2,1)S(1)}, u32[]{:S(2)}, u32[]{:S(2)}) collective-permute-start(bf16[16,128,128]{2,1,0:T(8,128)(2,1)} %get-tuple-element.278), channel_id=1, source_target_pairs={{0,2},{2,4},{4,6},{6,8},{8,10},{10,12},{12,14},{14,16},{16,18},{18... | collective-permute-start | bytes 1572872 | tf_op jit(solution)/shard_map/while/body/eval_jaxpr/ppermute | solution.py:16
  664.9 13.8 %collective-permute-start = (bf16[16,128,128]{2,1,0:T(8,128)(2,1)}, bf16[16,128,128]{2,1,0:T(8,128)(2,1)S(1)}, u32[]{:S(2)}, u32[]{:S(2)}) collective-permute-start(bf16[16,128,128]{2,1,0:T(8,128)(2,1)} %get-tuple-element.278), channel_id=1, source_target_pairs={{0,2},{2,4},{4,6},{6,8},{8,10},{10,12},{12,14},{14,16},{16,18},{18... | collective-permute-start | bytes 1572872 | tf_op jit(solution)/shard_map/while/body/eval_jaxpr/ppermute | solution.py:16
  682.4 15.1 %collective-permute-start = (bf16[16,128,128]{2,1,0:T(8,128)(2,1)}, bf16[16,128,128]{2,1,0:T(8,128)(2,1)S(1)}, u32[]{:S(2)}, u32[]{:S(2)}) collective-permute-start(bf16[16,128,128]{2,1,0:T(8,128)(2,1)} %get-tuple-element.278), channel_id=1, source_target_pairs={{0,2},{2,4},{4,6},{6,8},{8,10},{10,12},{12,14},{14,16},{16,18},{18... | collective-permute-start | bytes 1572872 | tf_op jit(solution)/shard_map/while/body/eval_jaxpr/ppermute | solution.py:16
  701.3 16.4 %collective-permute-start = (bf16[16,128,128]{2,1,0:T(8,128)(2,1)}, bf16[16,128,128]{2,1,0:T(8,128)(2,1)S(1)}, u32[]{:S(2)}, u32[]{:S(2)}) collective-permute-start(bf16[16,128,128]{2,1,0:T(8,128)(2,1)} %get-tuple-element.278), channel_id=1, source_target_pairs={{0,2},{2,4},{4,6},{6,8},{8,10},{10,12},{12,14},{14,16},{16,18},{18... | collective-permute-start | bytes 1572872 | tf_op jit(solution)/shard_map/while/body/eval_jaxpr/ppermute | solution.py:16
  721.5 17.5 %collective-permute-start = (bf16[16,128,128]{2,1,0:T(8,128)(2,1)}, bf16[16,128,128]{2,1,0:T(8,128)(2,1)S(1)}, u32[]{:S(2)}, u32[]{:S(2)}) collective-permute-start(bf16[16,128,128]{2,1,0:T(8,128)(2,1)} %get-tuple-element.278), channel_id=1, source_target_pairs={{0,2},{2,4},{4,6},{6,8},{8,10},{10,12},{12,14},{14,16},{16,18},{18... | collective-permute-start | bytes 1572872 | tf_op jit(solution)/shard_map/while/body/eval_jaxpr/ppermute | solution.py:16
  742.8 15.5 %copy-start.6 = (f32[128]{0:T(128)S(1)}, f32[128]{0:T(128)}, u32[]{:S(2)}) copy-start(f32[128]{0:T(128)} %param.24) | copy-start | bytes 1540
Sparse Core Ops, SparseCore 0:
  782.0 38.4 reduce-scatter.1
where the time goes:
time: 842 us; the launch traced here: 832 us
  matrix products  449 us (53%)
  waiting for transfers between devices  221 us (26%)
  other arithmetic  73.6 us (9%)
  local copies, waits for them, and re-layouts  49.6 us (6%)
  starting transfers between devices  23 us (3%)
  between operations  14 us (2%)
    ppermute x18, waiting for transfers between devices, from_behind(): lax.ppermute(value, axis, [(source, source + steps) for source in range(i...  183 us
    dot_general x5, matrix products, unit_inverse(): jnp.einsum('nhij,nhjk->nhik', inverse, identity_map + powered, precision=...  72.5 us
    dot_general x5, matrix products, unit_inverse(): jnp.einsum('nhij,nhjk->nhik', powered, powered, precision=exact_precision)  64.3 us
    dot_general x16, matrix products, advance(): jnp.einsum('hcd,hcw->hdw', carried_block, update, precision=exact_precision)  56.3 us
    dot_general x16, matrix products, advance(): jnp.einsum('hcm,hmw->hcw', score_block, update, precision=exact_precision)  49.3 us
    dot_general x16, matrix products, advance(): jnp.einsum('hcd,hdw->hcw', solved_block, carry_state, precision=exact_pre...  43.5 us
    dot_general x15, matrix products, batched(): return jnp.einsum('hij,hjk->hik', left, right, precision=exact_precision)  40.3 us
    reduce_scatter x1, waiting for transfers between devices, on_device(): lax.psum_scatter(jnp.dot(normed, out_weight, preferred_element_type=jnp.f...  38.6 us
  transfers between devices with their start and end apart: 19, of which 16 were waited for; matrix products, arithmetic and copies ran while one was open for 26% of the time, Pallas kernels for 0%

commit v1 on v0

--- a/solution.py
+++ b/solution.py
@@ -83,8 +83,9 @@
 
 
 def span_setup(queries, key_rows, values, log_gate, strength):
-    cumulative = jnp.cumsum(log_gate, axis=-1)
-    block_size = cumulative.shape[-1]
+    block_size = log_gate.shape[-1]
+    upper = jnp.triu(jnp.ones((block_size, block_size), jnp.float32))
+    cumulative = jnp.einsum("nhm,mc->nhc", log_gate, upper, precision=exact_precision)
     row_index = lax.broadcasted_iota(jnp.int32, (block_size, block_size), 0)
     col_index = lax.broadcasted_iota(jnp.int32, (block_size, block_size), 1)
     lower_mask = row_index >= col_index

time: 842 us -> 838 us (level)
  no operation moved by 1% of the time
where the time goes in v1:
time: 838 us; the launch traced here: 828 us
  matrix products  450 us (54%)
  waiting for transfers between devices  221 us (26%)
  other arithmetic  70.1 us (8%)
  local copies, waits for them, and re-layouts  49.5 us (6%)
  starting transfers between devices  23 us (3%)
  between operations  14 us (2%)
    ppermute x18, waiting for transfers between devices, from_behind(): lax.ppermute(value, axis, [(source, source + steps) for source in range(i...  182 us
    dot_general x5, matrix products, unit_inverse(): jnp.einsum('nhij,nhjk->nhik', inverse, identity_map + powered, precision=...  72.5 us
    dot_general x5, matrix products, unit_inverse(): jnp.einsum('nhij,nhjk->nhik', powered, powered, precision=exact_precision)  64.3 us
    dot_general x16, matrix products, advance(): jnp.einsum('hcd,hcw->hdw', carried_block, update, precision=exact_precision)  56.3 us
    dot_general x16, matrix products, advance(): jnp.einsum('hcm,hmw->hcw', score_block, update, precision=exact_precision)  49 us
    dot_general x16, matrix products, advance(): jnp.einsum('hcd,hdw->hcw', solved_block, carry_state, precision=exact_pre...  43.5 us
    dot_general x15, matrix products, batched(): return jnp.einsum('hij,hjk->hik', left, right, precision=exact_precision)  40.3 us
    reduce_scatter x1, waiting for transfers between devices, on_device(): lax.psum_scatter(jnp.dot(normed, out_weight, preferred_element_type=jnp.f...  38.6 us
  transfers between devices with their start and end apart: 19, of which 16 were waited for; matrix products, arithmetic and copies ran while one was open for 26% of the time, Pallas kernels for 0%

profile of v1, /device:TPU:31, one launch (start us, length us, event | category | flops | bytes accessed | tf_op | source)
XLA Modules:
  0.0 828.2 jit_solution(5234485682111591643)
XLA Ops:
  29.2 15.4 %fusion.43 = f32[16,16,64,64]{3,2,1,0:T(8,128)} fusion(f32[16,16,64,128]{3,2,0,1:T(8,128)S(1)} %bitcast.142), kind=kOutput, calls=%fused_computation.59 | convolution fusion | flops 1610612736 | bytes 12582912 | tf_op jit(solution)/shard_map/nhcd,nhmd->nhcm/dot_general | solution.py:95
  44.6 18.7 %fusion.45 = f32[16,16,64,64]{3,2,1,0:T(8,128)S(1)} fusion(f32[16,16,64,64]{3,2,1,0:T(8,128)} %fusion.43, f32[16,16,64]{2,1,0:T(8,128)S(1)} %convolution_bitcast_fusion, f32[16,16,64]{2,1,0:T(8,128)S(1)} %bitcast.153, pred[64,64]{1,0:T(8,128)(4,1)S(1)} %get-tuple-element.154, pred[64,64]{1,0:T(8,128)(4,1)S(1)} %get-tuple-element.155), kind=kOutput, calls=%fused_computation.61 | convolution fusion | flops 811597824 | bytes 8527872 | tf_op jit(solution)/shard_map/nhij,nhjk->nhik/dot_general | solution.py:77
  63.3 11.4 %fusion.103 = f32[16,16,64,64]{3,2,1,0:T(8,128)S(1)} fusion(f32[16,16,64,64]{3,2,1,0:T(8,128)S(1)} %fusion.45), kind=kOutput, calls=%fused_computation.157 | convolution fusion | flops 805306368 | bytes 8388608 | tf_op jit(solution)/shard_map/nhij,nhjk->nhik/dot_general | solution.py:77
  74.7 24.4 %fusion.39 = f32[16,16,64,64]{3,2,1,0:T(8,128)} fusion(f32[16,16,64,64]{3,2,1,0:T(8,128)S(1)} %fusion.45, f32[16,16,64,64]{3,2,1,0:T(8,128)} %fusion.43, f32[16,16,64]{2,1,0:T(8,128)S(1)} %convolution_bitcast_fusion, f32[16,16,64]{2,1,0:T(8,128)S(1)} %bitcast.154, f32[64,64]{1,0:T(8,128)S(1)} %fusion.90, pred[64,64]{1,0:T(8,128)(4,1)S(1)} %get-tuple-element.154, ...), kind=kOutput, calls=%fused_computation.53 | convolution fusion | flops 813694976 | bytes 12738560 | tf_op jit(solution)/shard_map/nhij,nhjk->nhik/dot_general | solution.py:78
  99.1 11.4 %fusion.104 = f32[16,16,64,64]{3,2,1,0:T(8,128)S(1)} fusion(f32[16,16,64,64]{3,2,1,0:T(8,128)S(1)} %fusion.103), kind=kOutput, calls=%fused_computation.158 | convolution fusion | flops 805306368 | bytes 8388608 | tf_op jit(solution)/shard_map/nhij,nhjk->nhik/dot_general | solution.py:77
  110.6 12.4 %fusion.37 = f32[16,16,64,64]{3,2,1,0:T(8,128)} fusion(f32[16,16,64,64]{3,2,1,0:T(8,128)} %fusion.39, f32[16,16,64,64]{3,2,1,0:T(8,128)S(1)} %fusion.103, f32[64,64]{1,0:T(8,128)S(1)} %fusion.90), kind=kOutput, calls=%fused_computation.51 | convolution fusion | flops 806354944 | bytes 12599296 | tf_op jit(solution)/shard_map/nhij,nhjk->nhik/dot_general | solution.py:78
  123.0 11.4 %fusion.105 = f32[16,16,64,64]{3,2,1,0:T(8,128)S(1)} fusion(f32[16,16,64,64]{3,2,1,0:T(8,128)S(1)} %fusion.104), kind=kOutput, calls=%fused_computation.159 | convolution fusion | flops 805306368 | bytes 8388608 | tf_op jit(solution)/shard_map/nhij,nhjk->nhik/dot_general | solution.py:77
  134.5 12.2 %fusion.35 = f32[16,16,64,64]{3,2,1,0:T(8,128)} fusion(f32[16,16,64,64]{3,2,1,0:T(8,128)} %fusion.37, f32[16,16,64,64]{3,2,1,0:T(8,128)S(1)} %fusion.104, f32[64,64]{1,0:T(8,128)S(1)} %fusion.90), kind=kOutput, calls=%fused_computation.49 | convolution fusion | flops 806354944 | bytes 12599296 | tf_op jit(solution)/shard_map/nhij,nhjk->nhik/dot_general | solution.py:78
  146.6 12.0 %fusion.33 = f32[16,16,64,64]{3,2,1,0:T(8,128)} fusion(f32[16,16,64,64]{3,2,1,0:T(8,128)} %fusion.35, f32[16,16,64,64]{3,2,1,0:T(8,128)S(1)} %fusion.105, f32[64,64]{1,0:T(8,128)S(1)} %fusion.90), kind=kOutput, calls=%fused_computation.47 | convolution fusion | flops 806354944 | bytes 12599296 | tf_op jit(solution)/shard_map/nhij,nhjk->nhik/dot_general | solution.py:78
  158.6 11.3 %fusion.106 = f32[16,16,64,64]{3,2,1,0:T(8,128)} fusion(f32[16,16,64,64]{3,2,1,0:T(8,128)S(1)} %fusion.105), kind=kOutput, calls=%fused_computation.160 | convolution fusion | flops 805306368 | bytes 8388608 | tf_op jit(solution)/shard_map/nhij,nhjk->nhik/dot_general | solution.py:77
  177.2 3.7 copy-done.2
  181.1 16.0 %multiply_select_fusion = f32[16,16,64,64]{3,2,1,0:T(8,128)} fusion(f32[16,16,64]{2,1,0:T(8,128)S(1)} %convolution_bitcast_fusion, pred[64,64]{1,0:T(8,128)(4,1)S(1)} %get-tuple-element.154, f32[16,16,64,128]{3,2,0,1:T(8,128)S(1)} %bitcast.145, f32[16,16,64,128]{3,2,0,1:T(8,128)S(1)} %bitcast.147), kind=kOutput, calls=%fused_computation.43 | convolution fusion | flops 1614807040 | bytes 21041152 | tf_op jit(solution)/shard_map/nhcd,nhmd->nhcm/dot_general | solution.py:99
  197.2 11.5 %fusion.31 = f32[16,16,64,64]{3,2,1,0:T(8,128)S(1)} fusion(f32[16,16,64,64]{3,2,1,0:T(8,128)} %fusion.33, f32[16,16,64,64]{3,2,1,0:T(8,128)} %fusion.106, f32[64,64]{1,0:T(8,128)S(1)} %fusion.90), kind=kOutput, calls=%fused_computation.45 | convolution fusion | flops 806354944 | bytes 12599296 | tf_op jit(solution)/shard_map/nhij,nhjk->nhik/dot_general | solution.py:78
  208.7 6.6 broadcast_multiply_fusion.1
  215.2 12.5 %fusion.26 = f32[16,16,64,128]{3,2,1,0:T(8,128)} fusion(f32[16,16,64,64]{3,2,1,0:T(8,128)S(1)} %fusion.31, f32[16,16,64,128]{3,2,0,1:T(8,128)} %get-tuple-element.134), kind=kOutput, calls=%fused_computation.38 | convolution fusion | flops 1610612736 | bytes 20971520 | tf_op jit(solution)/shard_map/nhcm,nhmd->nhcd/dot_general | solution.py:106
  227.7 4.6 broadcast_multiply_fusion
  232.9 7.2 constant_dynamic-update-slice_fusion.2
  240.1 15.8 %divide_multiply_fusion = f32[1024,16,128]{2,1,0:T(8,128)} fusion(f32[1027,16,128]{2,1,0:T(8,128)} %constant_dynamic-update-slice_fusion.2, f32[1024,16,128]{2,1,0:T(8,128)} %param.17, f32[16,128]{1,0:T(8,128)S(1)} %get-tuple-element.142, f32[16,128]{1,0:T(8,128)S(1)} %get-tuple-element.143, f32[16,128]{1,0:T(8,128)S(1)} %get-tuple-element.141, ...), kind=kLoop, calls=%fused_computation.44 | loop fusion | flops 23068672 | bytes 41975808 | tf_op jit(solution)/shard_map/jit(silu)/mul | solution.py:26
  256.0 14.3 %fusion.20 = f32[16,16,64,128]{3,2,1,0:T(8,128)} fusion(f32[16,16,64,64]{3,2,1,0:T(8,128)S(1)} %fusion.31, f32[16,64,16,128]{3,2,1,0:T(8,128)} %bitcast.149, f32[16,16,64]{2,1,0:T(8,128)S(1)} %bitcast.155), kind=kOutput, calls=%fused_computation.31 | convolution fusion | flops 1612709888 | bytes 21037056 | tf_op jit(solution)/shard_map/nhcm,nhmw->nhcw/dot_general | solution.py:103
  270.2 11.4 %concatenate.18 = f32[16,16,64,256]{3,2,1,0:T(8,128)} pad(f32[16,16,64,128]{3,2,1,0:T(8,128)} %fusion.20, f32[]{:T(128)} %constant.28.clone.1), padding=0_0x0_0x0_0x128_0 | pad | bytes 25165828 | tf_op jit(solution)/shard_map/concatenate | solution.py:188
  281.6 197.8 %while.24 = (s32[]{:T(128)}, f32[16,128,256]{2,1,0:T(8,128)S(1)}, f32[16,16,64,256]{3,2,0,1:T(8,128)}, f32[16,16]{1,0:T(8,128)}, f32[16,16,64,128]{3,2,0,1:T(8,1...) while((s32[]{:T(128)}, f32[16,128,256]{2,1,0:T(8,128)S(1)}, ...), condition=%wide.region_3.4_spmd, body=%wide.region_2.3_spmd.sunk | while | flops 1410859008 | bytes 17829160 | solution.py:132
  303.0 3.5 multiply_add_fusion.2
  327.7 3.5 multiply_add_fusion.2
  401.8 3.5 multiply_add_fusion.2
  438.8 3.5 multiply_add_fusion.2
  463.5 3.5 multiply_add_fusion.2
  475.9 3.5 multiply_add_fusion.2
  480.9 258.4 %while.25 = (s32[]{:T(128)}, f32[16,128,128]{2,1,0:T(8,128)}, bf16[16,128,128]{2,1,0:T(8,128)(2,1)}, f32[16,128,128]{2,1,0:T(8,128)}, f32[16,128,128]{2,1,0:T(8,128)S(1)}, /*index=5*/s32[]{:T(128)}) while((s32[]{:T(128)}, f32[16,128,128]{2,1,0:T(8,128)}, bf16[16,128,128]{2,1,0:T(8,128)(2,1)}, f32[16,128,128]{2,1,0:T(8,128)}, ...), condition=%wide.region_5.6_spmd, body=%wide.region_4.5_spmd.sunk | while | flops 403439616 | bytes 6815853 | solution.py:199
  482.2 15.5 %collective-permute-done = bf16[16,128,128]{2,1,0:T(8,128)(2,1)S(1)} collective-permute-done((bf16[16,128,128]{2,1,0:T(8,128)(2,1)}, bf16[16,128,128]{2,1,0:T(8,128)(2,1)S(1)}, u32[]{:S(2)}, u32[]{:S(2)}) %collective-permute-start) | collective-permute-done | bytes 524320 | tf_op jit(solution)/shard_map/while/body/eval_jaxpr/ppermute | solution.py:16
  502.8 13.2 %collective-permute-done = bf16[16,128,128]{2,1,0:T(8,128)(2,1)S(1)} collective-permute-done((bf16[16,128,128]{2,1,0:T(8,128)(2,1)}, bf16[16,128,128]{2,1,0:T(8,128)(2,1)S(1)}, u32[]{:S(2)}, u32[]{:S(2)}) %collective-permute-start) | collective-permute-done | bytes 524320 | tf_op jit(solution)/shard_map/while/body/eval_jaxpr/ppermute | solution.py:16
  521.1 12.3 %collective-permute-done = bf16[16,128,128]{2,1,0:T(8,128)(2,1)S(1)} collective-permute-done((bf16[16,128,128]{2,1,0:T(8,128)(2,1)}, bf16[16,128,128]{2,1,0:T(8,128)(2,1)S(1)}, u32[]{:S(2)}, u32[]{:S(2)}) %collective-permute-start) | collective-permute-done | bytes 524320 | tf_op jit(solution)/shard_map/while/body/eval_jaxpr/ppermute | solution.py:16
  538.4 11.4 %collective-permute-done = bf16[16,128,128]{2,1,0:T(8,128)(2,1)S(1)} collective-permute-done((bf16[16,128,128]{2,1,0:T(8,128)(2,1)}, bf16[16,128,128]{2,1,0:T(8,128)(2,1)S(1)}, u32[]{:S(2)}, u32[]{:S(2)}) %collective-permute-start) | collective-permute-done | bytes 524320 | tf_op jit(solution)/shard_map/while/body/eval_jaxpr/ppermute | solution.py:16
  554.9 10.5 %collective-permute-done = bf16[16,128,128]{2,1,0:T(8,128)(2,1)S(1)} collective-permute-done((bf16[16,128,128]{2,1,0:T(8,128)(2,1)}, bf16[16,128,128]{2,1,0:T(8,128)(2,1)S(1)}, u32[]{:S(2)}, u32[]{:S(2)}) %collective-permute-start) | collective-permute-done | bytes 524320 | tf_op jit(solution)/shard_map/while/body/eval_jaxpr/ppermute | solution.py:16
  570.5 9.5 %collective-permute-done = bf16[16,128,128]{2,1,0:T(8,128)(2,1)S(1)} collective-permute-done((bf16[16,128,128]{2,1,0:T(8,128)(2,1)}, bf16[16,128,128]{2,1,0:T(8,128)(2,1)S(1)}, u32[]{:S(2)}, u32[]{:S(2)}) %collective-permute-start) | collective-permute-done | bytes 524320 | tf_op jit(solution)/shard_map/while/body/eval_jaxpr/ppermute | solution.py:16
  585.0 9.9 %collective-permute-done = bf16[16,128,128]{2,1,0:T(8,128)(2,1)S(1)} collective-permute-done((bf16[16,128,128]{2,1,0:T(8,128)(2,1)}, bf16[16,128,128]{2,1,0:T(8,128)(2,1)S(1)}, u32[]{:S(2)}, u32[]{:S(2)}) %collective-permute-start) | collective-permute-done | bytes 524320 | tf_op jit(solution)/shard_map/while/body/eval_jaxpr/ppermute | solution.py:16
  599.9 10.2 %collective-permute-done = bf16[16,128,128]{2,1,0:T(8,128)(2,1)S(1)} collective-permute-done((bf16[16,128,128]{2,1,0:T(8,128)(2,1)}, bf16[16,128,128]{2,1,0:T(8,128)(2,1)S(1)}, u32[]{:S(2)}, u32[]{:S(2)}) %collective-permute-start) | collective-permute-done | bytes 524320 | tf_op jit(solution)/shard_map/while/body/eval_jaxpr/ppermute | solution.py:16
  615.1 10.6 %collective-permute-done = bf16[16,128,128]{2,1,0:T(8,128)(2,1)S(1)} collective-permute-done((bf16[16,128,128]{2,1,0:T(8,128)(2,1)}, bf16[16,128,128]{2,1,0:T(8,128)(2,1)S(1)}, u32[]{:S(2)}, u32[]{:S(2)}) %collective-permute-start) | collective-permute-done | bytes 524320 | tf_op jit(solution)/shard_map/while/body/eval_jaxpr/ppermute | solution.py:16
  630.8 10.6 %collective-permute-done = bf16[16,128,128]{2,1,0:T(8,128)(2,1)S(1)} collective-permute-done((bf16[16,128,128]{2,1,0:T(8,128)(2,1)}, bf16[16,128,128]{2,1,0:T(8,128)(2,1)S(1)}, u32[]{:S(2)}, u32[]{:S(2)}) %collective-permute-start) | collective-permute-done | bytes 524320 | tf_op jit(solution)/shard_map/while/body/eval_jaxpr/ppermute | solution.py:16
  646.5 11.1 %collective-permute-done = bf16[16,128,128]{2,1,0:T(8,128)(2,1)S(1)} collective-permute-done((bf16[16,128,128]{2,1,0:T(8,128)(2,1)}, bf16[16,128,128]{2,1,0:T(8,128)(2,1)S(1)}, u32[]{:S(2)}, u32[]{:S(2)}) %collective-permute-start) | collective-permute-done | bytes 524320 | tf_op jit(solution)/shard_map/while/body/eval_jaxpr/ppermute | solution.py:16
  662.7 12.5 %collective-permute-done = bf16[16,128,128]{2,1,0:T(8,128)(2,1)S(1)} collective-permute-done((bf16[16,128,128]{2,1,0:T(8,128)(2,1)}, bf16[16,128,128]{2,1,0:T(8,128)(2,1)S(1)}, u32[]{:S(2)}, u32[]{:S(2)}) %collective-permute-start) | collective-permute-done | bytes 524320 | tf_op jit(solution)/shard_map/while/body/eval_jaxpr/ppermute | solution.py:16
  680.3 13.8 %collective-permute-done = bf16[16,128,128]{2,1,0:T(8,128)(2,1)S(1)} collective-permute-done((bf16[16,128,128]{2,1,0:T(8,128)(2,1)}, bf16[16,128,128]{2,1,0:T(8,128)(2,1)S(1)}, u32[]{:S(2)}, u32[]{:S(2)}) %collective-permute-start) | collective-permute-done | bytes 524320 | tf_op jit(solution)/shard_map/while/body/eval_jaxpr/ppermute | solution.py:16
  699.1 15.1 %collective-permute-done = bf16[16,128,128]{2,1,0:T(8,128)(2,1)S(1)} collective-permute-done((bf16[16,128,128]{2,1,0:T(8,128)(2,1)}, bf16[16,128,128]{2,1,0:T(8,128)(2,1)S(1)}, u32[]{:S(2)}, u32[]{:S(2)}) %collective-permute-start) | collective-permute-done | bytes 524320 | tf_op jit(solution)/shard_map/while/body/eval_jaxpr/ppermute | solution.py:16
  719.3 16.2 %collective-permute-done = bf16[16,128,128]{2,1,0:T(8,128)(2,1)S(1)} collective-permute-done((bf16[16,128,128]{2,1,0:T(8,128)(2,1)}, bf16[16,128,128]{2,1,0:T(8,128)(2,1)S(1)}, u32[]{:S(2)}, u32[]{:S(2)}) %collective-permute-start) | collective-permute-done | bytes 524320 | tf_op jit(solution)/shard_map/while/body/eval_jaxpr/ppermute | solution.py:16
  739.3 15.2 %fusion.19 = (f32[16,64,16]{1,0,2:T(8,128)S(1)}, f32[16,16,64,128]{3,2,0,1:T(8,128)}) fusion(f32[16,16,64,256]{3,2,0,1:T(8,128)} %get-tuple-element.79, f32[16,128,128]{2,1,0:T(8,128)} %get-tuple-element.81), kind=kOutput, calls=%fused_computation.28 | convolution fusion | flops 3227500544 | bytes 26279936 | tf_op jit(solution)/shard_map/nhcd,hdw->nhcw/dot_general | solution.py:200
  754.8 11.0 %fusion.23 = bf16[1024,16,128]{2,1,0:T(8,128)(2,1)S(1)} fusion(f32[1024,16,128]{2,0,1:T(8,128)} %bitcast.150, f32[1024,16,128]{2,1,0:T(8,128)} %param.18, f32[128]{0:T(128)S(1)} %copy-done.6, f32[1024,16]{1,0:T(8,128)S(1)} %bitcast.152), kind=kLoop, calls=%fused_computation.35 | loop fusion | flops 16777216 | bytes 21037568 | tf_op jit(solution)/shard_map/convert_element_type | solution.py:206
  765.8 12.5 %fusion.75 = bf16[1024,2048]{1,0:T(8,128)(2,1)} fusion(bf16[2048,2048]{1,0:T(8,128)(2,1)} %param.25, bf16[128,8,16,128]{3,2,1,0:T(8,128)(2,1)S(1)} %bitcast.151), kind=kOutput, calls=%fused_computation.105 | convolution fusion | flops 8592031744 | bytes 16777216 | tf_op jit(solution)/shard_map/dot_general | solution.py:210
  778.4 38.6 %reduce-scatter.2.cloned.1.call-done = bf16[512,2048]{1,0:T(8,128)(2,1)} async-done(((bf16[1024,2048]{1,0:T(8,128)(2,1)}), bf16[512,2048]{1,0:T(8,128)(2,1)}) %reduce-scatter.2.cloned.1.call-update) | async-done | bytes 2097168 | tf_op jit(solution)/shard_map/reduce_scatter | solution.py:209
  817.0 4.1 convert_element_type.39
  (187 shorter events, 283.9 us)
Async XLA Ops:
  6.5 810.5 %reduce-scatter.2.cloned.1.call-start = ((), (), s32[]{:S(2)}) async-start(), calls=%async_computation.1 | async-start | bytes 6291456 | tf_op jit(solution)/shard_map/reduce_scatter | solution.py:209
  7.2 12.6 %collective-permute-start.1 = (f32[3,8,128]{2,1,0:T(8,128)S(1)}, f32[3,8,128]{2,1,0:T(8,128)S(1)}, u32[]{:S(2)}, u32[]{:S(2)}) collective-permute-start(f32[3,8,128]{2,1,0:T(8,128)S(1)} %slice.90), channel_id=1, source_target_pairs={{0,2},{2,4},{4,6},{6,8},{8,10},{10,12},{12,14},{14,16},{16,18},{18... | collective-permute-start | bytes 36872 | tf_op jit(solution)/shard_map/ppermute | solution.py:16
  9.3 223.0 %collective-permute-start.2 = (f32[3,16,128]{2,1,0:T(8,128)S(1)}, f32[3,16,128]{2,1,0:T(8,128)S(1)}, u32[]{:S(2)}, u32[]{:S(2)}) collective-permute-start(f32[3,16,128]{2,1,0:T(8,128)S(1)} %slice.98), channel_id=1, source_target_pairs={{0,2},{2,4},{4,6},{6,8},{8,10},{10,12},{12,14},{14,16},{16,18},{18... | collective-permute-start | bytes 73736 | tf_op jit(solution)/shard_map/ppermute | solution.py:16
  11.3 158.7 %collective-permute-start.3 = (f32[3,8,128]{2,1,0:T(8,128)S(1)}, f32[3,8,128]{2,1,0:T(8,128)S(1)}, u32[]{:S(2)}, u32[]{:S(2)}) collective-permute-start(f32[3,8,128]{2,1,0:T(8,128)S(1)} %slice.106), channel_id=1, source_target_pairs={{0,2},{2,4},{4,6},{6,8},{8,10},{10,12},{12,14},{14,16},{16,18},{18... | collective-permute-start | bytes 36872 | tf_op jit(solution)/shard_map/ppermute | solution.py:16
  18.2 4.5 copy-start.4
  29.2 15.4 %copy-start.1 = (f32[1024,8,2,128]{3,0,2,1:T(8,128)}, f32[1024,8,2,128]{3,0,2,1:T(8,128)S(1)}, u32[]{:S(2)}) copy-start(f32[1024,8,2,128]{3,0,2,1:T(8,128)S(1)} %broadcast_in_dim.67) | copy-start | bytes 25165828
  158.6 11.3 %copy-start.5 = (f32[1024,8,128]{2,1,0:T(8,128)S(1)}, f32[1024,8,128]{2,1,0:T(8,128)}, u32[]{:S(2)}) copy-start(f32[1024,8,128]{2,1,0:T(8,128)} %param.15) | copy-start | bytes 12582916
  175.5 5.4 slice-start
  176.3 4.8 slice-start.1
  177.2 3.7 copy-start.2
  215.2 12.5 %copy-start.3 = (f32[1024,8,2,128]{3,0,2,1:T(8,128)S(1)}, f32[1024,8,2,128]{3,0,2,1:T(8,128)}, u32[]{:S(2)}) copy-start(f32[1024,8,2,128]{3,0,2,1:T(8,128)} %copy-done.2) | copy-start | bytes 25165828
  270.2 11.4 %copy-start = (f32[16,128,256]{2,1,0:T(8,128)S(1)}, f32[16,128,256]{2,1,0:T(8,128)}, u32[]{:S(2)}) copy-start(f32[16,128,256]{2,1,0:T(8,128)} %concatenate.15) | copy-start | bytes 6291460
  481.0 16.8 %collective-permute-start = (bf16[16,128,128]{2,1,0:T(8,128)(2,1)}, bf16[16,128,128]{2,1,0:T(8,128)(2,1)S(1)}, u32[]{:S(2)}, u32[]{:S(2)}) collective-permute-start(bf16[16,128,128]{2,1,0:T(8,128)(2,1)} %get-tuple-element.278), channel_id=1, source_target_pairs={{0,2},{2,4},{4,6},{6,8},{8,10},{10,12},{12,14},{14,16},{16,18},{18... | collective-permute-start | bytes 1572872 | tf_op jit(solution)/shard_map/while/body/eval_jaxpr/ppermute | solution.py:16
  501.5 14.5 %collective-permute-start = (bf16[16,128,128]{2,1,0:T(8,128)(2,1)}, bf16[16,128,128]{2,1,0:T(8,128)(2,1)S(1)}, u32[]{:S(2)}, u32[]{:S(2)}) collective-permute-start(bf16[16,128,128]{2,1,0:T(8,128)(2,1)} %get-tuple-element.278), channel_id=1, source_target_pairs={{0,2},{2,4},{4,6},{6,8},{8,10},{10,12},{12,14},{14,16},{16,18},{18... | collective-permute-start | bytes 1572872 | tf_op jit(solution)/shard_map/while/body/eval_jaxpr/ppermute | solution.py:16
  519.8 13.6 %collective-permute-start = (bf16[16,128,128]{2,1,0:T(8,128)(2,1)}, bf16[16,128,128]{2,1,0:T(8,128)(2,1)S(1)}, u32[]{:S(2)}, u32[]{:S(2)}) collective-permute-start(bf16[16,128,128]{2,1,0:T(8,128)(2,1)} %get-tuple-element.278), channel_id=1, source_target_pairs={{0,2},{2,4},{4,6},{6,8},{8,10},{10,12},{12,14},{14,16},{16,18},{18... | collective-permute-start | bytes 1572872 | tf_op jit(solution)/shard_map/while/body/eval_jaxpr/ppermute | solution.py:16
  537.2 12.7 %collective-permute-start = (bf16[16,128,128]{2,1,0:T(8,128)(2,1)}, bf16[16,128,128]{2,1,0:T(8,128)(2,1)S(1)}, u32[]{:S(2)}, u32[]{:S(2)}) collective-permute-start(bf16[16,128,128]{2,1,0:T(8,128)(2,1)} %get-tuple-element.278), channel_id=1, source_target_pairs={{0,2},{2,4},{4,6},{6,8},{8,10},{10,12},{12,14},{14,16},{16,18},{18... | collective-permute-start | bytes 1572872 | tf_op jit(solution)/shard_map/while/body/eval_jaxpr/ppermute | solution.py:16
  553.6 11.8 %collective-permute-start = (bf16[16,128,128]{2,1,0:T(8,128)(2,1)}, bf16[16,128,128]{2,1,0:T(8,128)(2,1)S(1)}, u32[]{:S(2)}, u32[]{:S(2)}) collective-permute-start(bf16[16,128,128]{2,1,0:T(8,128)(2,1)} %get-tuple-element.278), channel_id=1, source_target_pairs={{0,2},{2,4},{4,6},{6,8},{8,10},{10,12},{12,14},{14,16},{16,18},{18... | collective-permute-start | bytes 1572872 | tf_op jit(solution)/shard_map/while/body/eval_jaxpr/ppermute | solution.py:16
  569.2 10.7 %collective-permute-start = (bf16[16,128,128]{2,1,0:T(8,128)(2,1)}, bf16[16,128,128]{2,1,0:T(8,128)(2,1)S(1)}, u32[]{:S(2)}, u32[]{:S(2)}) collective-permute-start(bf16[16,128,128]{2,1,0:T(8,128)(2,1)} %get-tuple-element.278), channel_id=1, source_target_pairs={{0,2},{2,4},{4,6},{6,8},{8,10},{10,12},{12,14},{14,16},{16,18},{18... | collective-permute-start | bytes 1572872 | tf_op jit(solution)/shard_map/while/body/eval_jaxpr/ppermute | solution.py:16
  583.7 11.2 %collective-permute-start = (bf16[16,128,128]{2,1,0:T(8,128)(2,1)}, bf16[16,128,128]{2,1,0:T(8,128)(2,1)S(1)}, u32[]{:S(2)}, u32[]{:S(2)}) collective-permute-start(bf16[16,128,128]{2,1,0:T(8,128)(2,1)} %get-tuple-element.278), channel_id=1, source_target_pairs={{0,2},{2,4},{4,6},{6,8},{8,10},{10,12},{12,14},{14,16},{16,18},{18... | collective-permute-start | bytes 1572872 | tf_op jit(solution)/shard_map/while/body/eval_jaxpr/ppermute | solution.py:16
  598.6 11.5 %collective-permute-start = (bf16[16,128,128]{2,1,0:T(8,128)(2,1)}, bf16[16,128,128]{2,1,0:T(8,128)(2,1)S(1)}, u32[]{:S(2)}, u32[]{:S(2)}) collective-permute-start(bf16[16,128,128]{2,1,0:T(8,128)(2,1)} %get-tuple-element.278), channel_id=1, source_target_pairs={{0,2},{2,4},{4,6},{6,8},{8,10},{10,12},{12,14},{14,16},{16,18},{18... | collective-permute-start | bytes 1572872 | tf_op jit(solution)/shard_map/while/body/eval_jaxpr/ppermute | solution.py:16
  613.9 11.9 %collective-permute-start = (bf16[16,128,128]{2,1,0:T(8,128)(2,1)}, bf16[16,128,128]{2,1,0:T(8,128)(2,1)S(1)}, u32[]{:S(2)}, u32[]{:S(2)}) collective-permute-start(bf16[16,128,128]{2,1,0:T(8,128)(2,1)} %get-tuple-element.278), channel_id=1, source_target_pairs={{0,2},{2,4},{4,6},{6,8},{8,10},{10,12},{12,14},{14,16},{16,18},{18... | collective-permute-start | bytes 1572872 | tf_op jit(solution)/shard_map/while/body/eval_jaxpr/ppermute | solution.py:16
  629.5 11.9 %collective-permute-start = (bf16[16,128,128]{2,1,0:T(8,128)(2,1)}, bf16[16,128,128]{2,1,0:T(8,128)(2,1)S(1)}, u32[]{:S(2)}, u32[]{:S(2)}) collective-permute-start(bf16[16,128,128]{2,1,0:T(8,128)(2,1)} %get-tuple-element.278), channel_id=1, source_target_pairs={{0,2},{2,4},{4,6},{6,8},{8,10},{10,12},{12,14},{14,16},{16,18},{18... | collective-permute-start | bytes 1572872 | tf_op jit(solution)/shard_map/while/body/eval_jaxpr/ppermute | solution.py:16
  645.2 12.4 %collective-permute-start = (bf16[16,128,128]{2,1,0:T(8,128)(2,1)}, bf16[16,128,128]{2,1,0:T(8,128)(2,1)S(1)}, u32[]{:S(2)}, u32[]{:S(2)}) collective-permute-start(bf16[16,128,128]{2,1,0:T(8,128)(2,1)} %get-tuple-element.278), channel_id=1, source_target_pairs={{0,2},{2,4},{4,6},{6,8},{8,10},{10,12},{12,14},{14,16},{16,18},{18... | collective-permute-start | bytes 1572872 | tf_op jit(solution)/shard_map/while/body/eval_jaxpr/ppermute | solution.py:16
  661.4 13.8 %collective-permute-start = (bf16[16,128,128]{2,1,0:T(8,128)(2,1)}, bf16[16,128,128]{2,1,0:T(8,128)(2,1)S(1)}, u32[]{:S(2)}, u32[]{:S(2)}) collective-permute-start(bf16[16,128,128]{2,1,0:T(8,128)(2,1)} %get-tuple-element.278), channel_id=1, source_target_pairs={{0,2},{2,4},{4,6},{6,8},{8,10},{10,12},{12,14},{14,16},{16,18},{18... | collective-permute-start | bytes 1572872 | tf_op jit(solution)/shard_map/while/body/eval_jaxpr/ppermute | solution.py:16
  679.0 15.1 %collective-permute-start = (bf16[16,128,128]{2,1,0:T(8,128)(2,1)}, bf16[16,128,128]{2,1,0:T(8,128)(2,1)S(1)}, u32[]{:S(2)}, u32[]{:S(2)}) collective-permute-start(bf16[16,128,128]{2,1,0:T(8,128)(2,1)} %get-tuple-element.278), channel_id=1, source_target_pairs={{0,2},{2,4},{4,6},{6,8},{8,10},{10,12},{12,14},{14,16},{16,18},{18... | collective-permute-start | bytes 1572872 | tf_op jit(solution)/shard_map/while/body/eval_jaxpr/ppermute | solution.py:16
  697.8 16.4 %collective-permute-start = (bf16[16,128,128]{2,1,0:T(8,128)(2,1)}, bf16[16,128,128]{2,1,0:T(8,128)(2,1)S(1)}, u32[]{:S(2)}, u32[]{:S(2)}) collective-permute-start(bf16[16,128,128]{2,1,0:T(8,128)(2,1)} %get-tuple-element.278), channel_id=1, source_target_pairs={{0,2},{2,4},{4,6},{6,8},{8,10},{10,12},{12,14},{14,16},{16,18},{18... | collective-permute-start | bytes 1572872 | tf_op jit(solution)/shard_map/while/body/eval_jaxpr/ppermute | solution.py:16
  718.0 17.5 %collective-permute-start = (bf16[16,128,128]{2,1,0:T(8,128)(2,1)}, bf16[16,128,128]{2,1,0:T(8,128)(2,1)S(1)}, u32[]{:S(2)}, u32[]{:S(2)}) collective-permute-start(bf16[16,128,128]{2,1,0:T(8,128)(2,1)} %get-tuple-element.278), channel_id=1, source_target_pairs={{0,2},{2,4},{4,6},{6,8},{8,10},{10,12},{12,14},{14,16},{16,18},{18... | collective-permute-start | bytes 1572872 | tf_op jit(solution)/shard_map/while/body/eval_jaxpr/ppermute | solution.py:16
  739.3 15.5 %copy-start.6 = (f32[128]{0:T(128)S(1)}, f32[128]{0:T(128)}, u32[]{:S(2)}) copy-start(f32[128]{0:T(128)} %param.24) | copy-start | bytes 1540
Sparse Core Ops, SparseCore 0:
  778.5 38.4 reduce-scatter.1

commit v2 on v0

v2 whole, which is shorter than its diff:
```python
import functools

import jax
import jax.numpy as jnp
from jax import lax
from jax.experimental import pallas as pl
from jax.experimental.pallas import tpu as pltpu
from jax.sharding import PartitionSpec as P

norm_epsilon = 1e-06
CHUNK = 128
BASE = 32
RIM = 8
VMEM_LIMIT = 56 * 2**20


def mm(left, right):
    return jnp.dot(
        left.astype(jnp.bfloat16), right.astype(jnp.bfloat16), preferred_element_type=jnp.float32
    )


def silu(value):
    return value / (1.0 + jnp.exp(-value))


def from_behind(value, axis, steps):
    count = lax.axis_size(axis)
    return lax.ppermute(value, axis, [(s, s + steps) for s in range(max(0, count - steps))])


def conv_head(x_ref, rim_ref, w_ref, head, heads, chunk, taps):
    current = x_ref[pl.ds(head, chunk, stride=heads), :]
    padded = jnp.concatenate([rim_ref[pl.ds(head, RIM, stride=heads), :], current], axis=0)
    total = w_ref[(taps - 1) * heads + head : (taps - 1) * heads + head + 1, :] * current
    for back in range(1, taps):
        row = (taps - 1 - back) * heads + head
        total = total + w_ref[row : row + 1, :] * pltpu.roll(padded, back, 0)[RIM:]
    return silu(total)


def unit_rows(matrix, scale=1.0):
    total = jnp.sum(matrix * matrix, axis=-1, keepdims=True)
    return matrix * (lax.rsqrt(total + norm_epsilon) * scale)


def chunk_kernel(
    meta,
    q_ref,
    k_ref,
    v_ref,
    q_rim,
    k_rim,
    v_rim,
    q_w,
    k_w,
    v_w,
    crow_ref,
    ccol_ref,
    bcol_ref,
    out_ref,
    fin_ref,
    state,
    q_old,
    k_old,
    v_old,
):
    chunk, kheads, vheads, kfirst, kgroup, taps = meta
    ratio = vheads // kheads
    width = q_ref.shape[1]
    step = pl.program_id(0)

    @pl.when(step == 0)
    def _():
        q_old[...] = q_rim[...]
        k_old[...] = k_rim[...]
        v_old[...] = v_rim[...]
        row = lax.broadcasted_iota(jnp.int32, (width, 2 * width), 0)
        col = lax.broadcasted_iota(jnp.int32, (width, 2 * width), 1)
        start = jnp.where(row == col, 1.0, 0.0)
        for v in range(kgroup * ratio):
            state[v] = start

    row = lax.broadcasted_iota(jnp.int32, (chunk, chunk), 0)
    col = lax.broadcasted_iota(jnp.int32, (chunk, chunk), 1)
    lower = row >= col
    strict = row > col
    eye = jnp.where(row == col, 1.0, 0.0)

    def same(size):
        return (row // size) == (col // size)

    count = kgroup * ratio
    keys, keys_t, lifted, scores, mixing, rhs = [], [], [], [], [], []
    for i in range(kgroup):
        q = unit_rows(conv_head(q_ref, q_old, q_w, kfirst + i, kheads, chunk, taps), width**-0.5)
        k = unit_rows(conv_head(k_ref, k_old, k_w, kfirst + i, kheads, chunk, taps))
        k_t = k.T.astype(jnp.bfloat16)
        inner = mm(k, k_t)
        cross = mm(q, k_t)
        for r in range(ratio):
            v = i * ratio + r
            values = conv_head(v_ref, v_old, v_w, kfirst * ratio + v, vheads, chunk, taps)
            cc = ccol_ref[:, v : v + 1]
            b = bcol_ref[:, v : v + 1]
            decay = jnp.exp(jnp.minimum(cc - crow_ref[v : v + 1, :], 0.0))
            lift = jnp.exp(cc)
            mixing.append(jnp.where(strict, -(b * inner * decay), 0.0))
            scores.append(jnp.where(lower, cross * decay, 0.0).astype(jnp.bfloat16))
            lifted.append((lift * q).astype(jnp.bfloat16))
            rhs.append(
                jnp.concatenate([b * values, (b * lift) * k], axis=1).astype(jnp.bfloat16)
            )
            keys_t.append(k_t)

    base = min(BASE, chunk)
    near = same(base)
    power = [jnp.where(near, m, 0.0).astype(jnp.bfloat16) for m in mixing]
    inverse = [eye + p.astype(jnp.float32) for p in power]
    power = [mm(p, p).astype(jnp.bfloat16) for p in power]
    reach = 2
    while reach < base:
        if reach * 2 < base:
            both = [
                mm(jnp.concatenate([t.astype(jnp.bfloat16), p], axis=0), p)
                for t, p in zip(inverse, power)
            ]
            inverse = [t + x[:chunk] for t, x in zip(inverse, both)]
            power = [x[chunk:].astype(jnp.bfloat16) for x in both]
        else:
            inverse = [t + mm(t, p) for t, p in zip(inverse, power)]
        reach *= 2
    size = base
    while size < chunk:
        far = same(2 * size) & jnp.logical_not(same(size))
        halves = [t.astype(jnp.bfloat16) for t in inverse]
        links = [mm(jnp.where(far, m, 0.0), t) for m, t in zip(mixing, halves)]
        inverse = [t + mm(h, x) for t, h, x in zip(inverse, halves, links)]
        size *= 2

    solved = [mm(t, r) for t, r in zip(inverse, rhs)]
    states = [state[v] for v in range(count)]
    narrow = [s.astype(jnp.bfloat16) for s in states]
    taken = [mm(x[:, width:], s) for x, s in zip(solved, narrow)]
    update = [
        jnp.concatenate([-w[:, :width], x[:, :width] - w[:, width:]], axis=1)
        for w, x in zip(taken, solved)
    ]
    for v in range(count):
        left = jnp.concatenate([lifted[v], scores[v]], axis=1)
        right = jnp.concatenate([narrow[v], update[v].astype(jnp.bfloat16)], axis=0)
        out_ref[v] = mm(left, right).astype(out_ref.dtype)
        last = crow_ref[v : v + 1, chunk - 1 : chunk]
        fade = jnp.exp(last - ccol_ref[:, v : v + 1])
        state[v] = jnp.exp(last) * states[v] + mm(keys_t[v], fade * update[v])

    for old, ref, heads in ((q_old, q_ref, kheads), (k_old, k_ref, kheads), (v_old, v_ref, vheads)):
        old[...] = ref[(chunk - RIM) * heads : chunk * heads, :]

    @pl.when(step == pl.num_programs(0) - 1)
    def _():
        fin_ref[...] = state[...]


def chunk_call(meta, tokens, width, arrays):
    chunk, kheads, vheads, kfirst, kgroup, taps = meta
    count = kgroup * (vheads // kheads)
    group = kfirst // kgroup

    def whole(rows):
        return pl.BlockSpec((rows, width), lambda c: (0, 0))

    def part(rows):
        return pl.BlockSpec((rows, width), lambda c: (c, 0))

    flops = 2 * tokens * count * width * width * 20
    return pl.pallas_call(
        functools.partial(chunk_kernel, meta),
        grid=(tokens // chunk,),
        in_specs=[
            part(chunk * kheads),
            part(chunk * kheads),
            part(chunk * vheads),
            whole(RIM * kheads),
            whole(RIM * kheads),
            whole(RIM * vheads),
            whole(taps * kheads),
            whole(taps * kheads),
            whole(taps * vheads),
            pl.BlockSpec((count, chunk), lambda c: (group, c)),
            pl.BlockSpec((chunk, count), lambda c: (c, 0)),
            pl.BlockSpec((chunk, count), lambda c: (c, 0)),
        ],
        out_specs=[
            pl.BlockSpec((count, chunk, 2 * width), lambda c: (0, c, 0)),
            pl.BlockSpec((count, width, 2 * width), lambda c: (0, 0, 0)),
        ],
        out_shape=[
            jax.ShapeDtypeStruct((count, tokens, 2 * width), jnp.bfloat16),
            jax.ShapeDtypeStruct((count, width, 2 * width), jnp.float32),
        ],
        scratch_shapes=[
            pltpu.VMEM((count, width, 2 * width), jnp.float32),
            pltpu.VMEM((RIM * kheads, width), jnp.float32),
            pltpu.VMEM((RIM * kheads, width), jnp.float32),
            pltpu.VMEM((RIM * vheads, width), jnp.float32),
        ],
        compiler_params=pltpu.CompilerParams(
            dimension_semantics=("arbitrary",), vmem_limit_bytes=VMEM_LIMIT
        ),
        cost_estimate=pl.CostEstimate(
            flops=flops, bytes_accessed=24 * 2**20, transcendentals=tokens * count * width * 4
        ),
    )(*arrays)


def enter_state(final):
    width = final.shape[1]

    def compose(later, earlier):
        return jnp.einsum(
            "hij,hjk->hik",
            later[:, :, :width].astype(jnp.bfloat16),
            earlier,
            preferred_element_type=jnp.float32,
        )

    count = lax.axis_size("ctx")
    empty = jnp.zeros((final.shape[0], width, width), jnp.float32)
    pair, reach = final, 1
    while 2 * reach < count:
        earlier = from_behind(pair.astype(jnp.bfloat16), "ctx", reach)
        pair = compose(pair, earlier) + jnp.concatenate([empty, pair[:, :, width:]], axis=2)
        reach *= 2
    sent = pair.astype(jnp.bfloat16)
    near = from_behind(sent, "ctx", 1)
    far = from_behind(sent[:, :, width:], "ctx", reach + 1)
    return (compose(near, far) + near[:, :, width:].astype(jnp.float32)).astype(jnp.bfloat16)


def mix_kernel(groups, rows, vheads, first_ref, *refs):
    outs, enters = refs[:groups], refs[groups : 2 * groups]
    gate_ref, gain_ref, weight_ref, part_ref, normed = refs[2 * groups :]
    width = gain_ref.shape[1]
    count = vheads // groups
    for g in range(groups):
        for v in range(count):
            head = g * count + v
            own = outs[g][v]
            recurrent = own[:, width:].astype(jnp.float32) + mm(own[:, :width], enters[g][v])
            mean = jnp.sum(recurrent * recurrent, axis=-1, keepdims=True) * (1.0 / width)
            gate = gate_ref[pl.ds(head, rows, stride=vheads), :]
            scaled = recurrent * lax.rsqrt(mean + norm_epsilon) * gain_ref[...] * silu(gate)
            normed[:, head * width : (head + 1) * width] = scaled.astype(jnp.bfloat16)
    depth, columns = weight_ref.shape
    piece = min(512, columns)
    for c in range(0, columns, piece):
        part_ref[:, c : c + piece] = jnp.dot(
            normed[...], weight_ref[:, c : c + piece], preferred_element_type=jnp.float32
        ).astype(jnp.bfloat16)


def mix_call(first, tokens, outs, enters, gate, gain, weight):
    groups = len(outs)
    count, all_tokens, double = outs[0].shape
    width = double // 2
    vheads = gate.shape[0] // all_tokens
    rows = min(256, tokens)
    depth, columns = weight.shape
    spec = pltpu.PrefetchScalarGridSpec(
        num_scalar_prefetch=1,
        grid=(tokens // rows,),
        in_specs=[pl.BlockSpec((count, rows, double), lambda t, s: (0, s[0] + t, 0))] * groups
        + [pl.BlockSpec((count, width, width), lambda t, s: (0, 0, 0))] * groups
        + [
            pl.BlockSpec((rows * vheads, width), lambda t, s: (s[0] + t, 0)),
            pl.BlockSpec((1, width), lambda t, s: (0, 0)),
            pl.BlockSpec((depth, columns), lambda t, s: (0, 0)),
        ],
        out_specs=pl.BlockSpec((rows, columns), lambda t, s: (t, 0)),
        scratch_shapes=[pltpu.VMEM((rows, depth), jnp.bfloat16)],
    )
    return pl.pallas_call(
        functools.partial(mix_kernel, groups, rows, vheads),
        grid_spec=spec,
        out_shape=jax.ShapeDtypeStruct((tokens, columns), jnp.bfloat16),
        compiler_params=pltpu.CompilerParams(
            dimension_semantics=("arbitrary",), vmem_limit_bytes=VMEM_LIMIT
        ),
        cost_estimate=pl.CostEstimate(
            flops=2 * tokens * depth * columns,
            bytes_accessed=2 * depth * columns + 16 * tokens * depth,
            transcendentals=tokens * depth,
        ),
    )((first // rows).astype(jnp.int32).reshape(1), *outs, *enters, gate, gain, weight)


def on_device(
    query_in,
    key_in,
    value_in,
    gate_in,
    log_gate,
    strength,
    query_conv,
    key_conv,
    value_conv,
    norm_gain,
    out_weight,
):
    tokens, kheads, width = query_in.shape
    vheads = value_in.shape[1]
    taps = query_conv.shape[0]
    ratio = vheads // kheads
    chunk = min(CHUNK, tokens)
    rim = taps - 1

    def flat(array):
        return array.reshape(-1, width)

    rims = from_behind(
        jnp.concatenate([a[-rim:] for a in (query_in, key_in, value_in)], axis=1), "ctx", 1
    )
    rims = jnp.pad(rims, ((RIM - rim, 0), (0, 0), (0, 0)))
    q_rim, k_rim, v_rim = (
        flat(rims[:, a:b])
        for a, b in ((0, kheads), (kheads, 2 * kheads), (2 * kheads, 2 * kheads + vheads))
    )
    upper = jnp.triu(jnp.ones((chunk, chunk), jnp.float32))
    summed = jnp.einsum(
        "hnm,mc->hnc",
        log_gate.reshape(vheads, tokens // chunk, chunk),
        upper,
        precision=lax.Precision.HIGHEST,
    ).reshape(vheads, tokens)

    kgroup = min(4, kheads)
    outs, enters = [], []
    for kfirst in range(0, kheads, kgroup):
        picked = slice(kfirst * ratio, (kfirst + kgroup) * ratio)
        out, final = chunk_call(
            (chunk, kheads, vheads, kfirst, kgroup, taps),
            tokens,
            width,
            (
                flat(query_in),
                flat(key_in),
                flat(value_in),
                q_rim,
                k_rim,
                v_rim,
                flat(query_conv),
                flat(key_conv),
                flat(value_conv),
                summed,
                summed[picked].T,
                strength[picked].T,
            ),
        )
        outs.append(out)
        enters.append(enter_state(final))

    shares = lax.axis_size("head")
    gate = flat(gate_in)
    gain = norm_gain.reshape(1, width)
    mix = functools.partial(
        mix_call, outs=outs, enters=enters, gate=gate, gain=gain, weight=out_weight
    )
    if shares != 2:
        partial = mix(jnp.int32(0), tokens)
        return lax.psum_scatter(partial, "head", scatter_dimension=0, tiled=True).astype(
            jnp.float32
        )
    me = lax.axis_index("head")
    half = tokens // 2
    other = mix((1 - me) * half, half)
    arrived = lax.ppermute(other, "head", [(0, 1), (1, 0)])
    own = mix(me * half, half)
    return own.astype(jnp.float32) + arrived.astype(jnp.float32)


def solution(mesh):
    in_specs = (
        P("ctx", "head", None),
        P("ctx", "head", None),
        P("ctx", "head", None),
        P("ctx", "head", None),
        P("head", "ctx"),
        P("head", "ctx"),
        P(None, "head", None),
        P(None, "head", None),
        P(None, "head", None),
        P(),
        P("head", None),
    )
    out_specs = P(("ctx", "head"), None)
    return jax.shard_map(
        on_device, mesh=mesh, in_specs=in_specs, out_specs=out_specs, check_vma=False
    )
```

time: 842 us -> 207 us (0.25)
  the two profiles are of different devices: /device:TPU:31 before, /device:TPU:17 now
where the time goes in v2:
time: 207 us; the launch traced here: 206 us
  Pallas kernels  83.3 us (40%)
  waiting for transfers between devices  55.5 us (27%)
  starting transfers between devices  46.4 us (22%)
  local copies, waits for them, and re-layouts  10.2 us (5%)
  other arithmetic  6.93 us (3%)
  matrix products  3.85 us (2%)
    pallas_call x2, Pallas kernels, chunk_call(): pl.pallas_call(functools.partial(chunk_kernel, meta), grid=(tokens // chu...  57.3 us
    ppermute x11, waiting for transfers between devices, from_behind(): lax.ppermute(value, axis, [(s, s + steps) for s in range(max(0, count - s...  55.5 us
    ppermute x11, starting transfers between devices, from_behind(): lax.ppermute(value, axis, [(s, s + steps) for s in range(max(0, count - s...  33.1 us
    pallas_call x2, Pallas kernels, mix_call(): pl.pallas_call(functools.partial(mix_kernel, groups, rows, vheads), grid_...  26 us
    ppermute x1, starting transfers between devices, on_device(): arrived = lax.ppermute(other, 'head', [(0, 1), (1, 0)])  13.3 us
    add x1, other arithmetic, on_device(): return own.astype(jnp.float32) + arrived.astype(jnp.float32)  4.36 us
  transfers between devices with their start and end apart: 12, of which 6 were waited for; matrix products, arithmetic and copies ran while one was open for 5% of the time, Pallas kernels for 20%

profile of v2, /device:TPU:17, one launch (start us, length us, event | category | flops | bytes accessed | tf_op | source)
XLA Modules:
  0.0 206.5 jit_solution(5994032838865841943)
XLA Ops:
  0.0 0.7 slice.96
  0.7 0.7 slice.97
  1.5 0.7 slice.98
  2.2 3.1 %collective-permute-start = (f32[3,32,128]{2,1,0:T(8,128)S(1)}, f32[3,32,128]{2,1,0:T(8,128)S(1)}, u32[]{:S(2)}, u32[]{:S(2)}) collective-permute-start(f32[3,32,128]{2,1,0:T(8,128)S(1)} %pad_maximum_fusion), channel_id=1, source_target_pairs={{0,2},{2,4},{4,6},{6,8},{8,10},{10,12},{12,14},{14,16},{16,18},{18... | collective-permute-start | bytes 147464 | tf_op jit(solution)/shard_map/ppermute | solution.py:29
  5.3 0.3 fusion.12
  5.6 0.6 copy_bitcast_fusion.crow_ref
  6.2 0.8 fusion.24
  7.0 1.0 copy.17
  8.0 1.0 copy.16
  9.0 1.0 copy.15
  10.0 1.0 copy.14
  11.1 0.6 pad_slice_fusion
  11.7 0.6 fusion.18
  12.3 28.6 %shard_map.109 = (bf16[8,1024,256]{2,1,0:T(8,128)(2,1)}, f32[8,128,256]{2,1,0:T(8,128)}) custom-call(f32[8192,128]{1,0:T(8,128)} %bitcast.60, f32[8192,128]{1,0:T(8,128)} %bitcast.62, f32[16384,128]{1,0:T(8,128)} %bitcast.58, f32[64,128]{1,0:T(8,128)} %get-tuple-element.18.q_rim, f32[64,128]{1,0:T(8,128)} %get-tuple-element.17.k_rim, f32[128,128]{1,0:T(8,128)} %bitcast.54, ...), custom_call_target="tpu_custom_call" | custom-call | flops 5368709120 | bytes 25165824 | tf_op jit(solution)/shard_map/pallas_call | solution.py:177
  40.9 1.3 convert.18
  42.2 3.1 %collective-permute-start.1 = (bf16[8,128,256]{2,1,0:T(8,128)(2,1)S(1)}, bf16[8,128,256]{2,1,0:T(8,128)(2,1)S(1)}, u32[]{:S(2)}, u32[]{:S(2)}) collective-permute-start(bf16[8,128,256]{2,1,0:T(8,128)(2,1)S(1)} %convert.18), channel_id=1, source_target_pairs={{0,2},{2,4},{4,6},{6,8},{8,10},{10,12},{12,14},{14,16},{16,18},{18... | collective-permute-start | bytes 1572872 | tf_op jit(solution)/shard_map/ppermute | solution.py:29
  45.3 28.7 %shard_map.110 = (bf16[8,1024,256]{2,1,0:T(8,128)(2,1)}, f32[8,128,256]{2,1,0:T(8,128)}) custom-call(f32[8192,128]{1,0:T(8,128)} %bitcast.61, f32[8192,128]{1,0:T(8,128)} %bitcast.63, f32[16384,128]{1,0:T(8,128)} %bitcast.59, f32[64,128]{1,0:T(8,128)} %get-tuple-element.18.q_rim, f32[64,128]{1,0:T(8,128)} %get-tuple-element.17.k_rim, f32[128,128]{1,0:T(8,128)} %bitcast.55, ...), custom_call_target="tpu_custom_call" | custom-call | flops 5368709120 | bytes 25165824 | tf_op jit(solution)/shard_map/pallas_call | solution.py:177
  74.0 1.3 convert.21
  75.3 3.1 %collective-permute-start.6 = (bf16[8,128,256]{2,1,0:T(8,128)(2,1)S(1)}, bf16[8,128,256]{2,1,0:T(8,128)(2,1)S(1)}, u32[]{:S(2)}, u32[]{:S(2)}) collective-permute-start(bf16[8,128,256]{2,1,0:T(8,128)(2,1)S(1)} %convert.21), channel_id=1, source_target_pairs={{0,2},{2,4},{4,6},{6,8},{8,10},{10,12},{12,14},{14,16},{16,18},{18... | collective-permute-start | bytes 1572872 | tf_op jit(solution)/shard_map/ppermute | solution.py:29
  78.4 1.1 slice.118
  79.5 0.0 collective-permute-done.1
  79.5 0.3 fusion.26
  79.8 3.2 %collective-permute-start.2 = (bf16[8,128,256]{2,1,0:T(8,128)(2,1)S(1)}, bf16[8,128,256]{2,1,0:T(8,128)(2,1)S(1)}, u32[]{:S(2)}, u32[]{:S(2)}) collective-permute-start(bf16[8,128,256]{2,1,0:T(8,128)(2,1)S(1)} %get-tuple-element.19), channel_id=1, source_target_pairs={{0,4},{2,6},{4,8},{6,10},{8,12},{10,14},{12,16},{14,18},{16,20},{1... | collective-permute-start | bytes 1572872 | tf_op jit(solution)/shard_map/ppermute | solution.py:29
  83.0 12.7 %collective-permute-done.6 = bf16[8,128,256]{2,1,0:T(8,128)(2,1)S(1)} collective-permute-done((bf16[8,128,256]{2,1,0:T(8,128)(2,1)S(1)}, bf16[8,128,256]{2,1,0:T(8,128)(2,1)S(1)}, u32[]{:S(2)}, u32[]{:S(2)}) %collective-permute-start.6) | collective-permute-done | bytes 524320 | tf_op jit(solution)/shard_map/ppermute | solution.py:29
  95.7 0.3 fusion.28
  96.0 1.9 collective-permute-start.7
  98.0 4.5 %collective-permute-done.2 = bf16[8,128,256]{2,1,0:T(8,128)(2,1)S(1)} collective-permute-done((bf16[8,128,256]{2,1,0:T(8,128)(2,1)S(1)}, bf16[8,128,256]{2,1,0:T(8,128)(2,1)S(1)}, u32[]{:S(2)}, u32[]{:S(2)}) %collective-permute-start.2) | collective-permute-done | bytes 524320 | tf_op jit(solution)/shard_map/ppermute | solution.py:29
  102.5 0.3 fusion.27
  102.8 3.2 %collective-permute-start.3 = (bf16[8,128,256]{2,1,0:T(8,128)(2,1)S(1)}, bf16[8,128,256]{2,1,0:T(8,128)(2,1)S(1)}, u32[]{:S(2)}, u32[]{:S(2)}) collective-permute-start(bf16[8,128,256]{2,1,0:T(8,128)(2,1)S(1)} %get-tuple-element.21), channel_id=1, source_target_pairs={{0,8},{2,10},{4,12},{6,14},{8,16},{10,18},{12,20},{14,22},{16,24},... | collective-permute-start | bytes 1572872 | tf_op jit(solution)/shard_map/ppermute | solution.py:29
  106.0 7.4 %collective-permute-done.7 = bf16[8,128,256]{2,1,0:T(8,128)(2,1)S(1)} collective-permute-done((bf16[8,128,256]{2,1,0:T(8,128)(2,1)S(1)}, bf16[8,128,256]{2,1,0:T(8,128)(2,1)S(1)}, u32[]{:S(2)}, u32[]{:S(2)}) %collective-permute-start.7) | collective-permute-done | bytes 524320 | tf_op jit(solution)/shard_map/ppermute | solution.py:29
  113.4 0.3 fusion.29
  113.7 3.2 %collective-permute-start.8 = (bf16[8,128,256]{2,1,0:T(8,128)(2,1)S(1)}, bf16[8,128,256]{2,1,0:T(8,128)(2,1)S(1)}, u32[]{:S(2)}, u32[]{:S(2)}) collective-permute-start(bf16[8,128,256]{2,1,0:T(8,128)(2,1)S(1)} %get-tuple-element.25), channel_id=1, source_target_pairs={{0,8},{2,10},{4,12},{6,14},{8,16},{10,18},{12,20},{14,22},{16,24},... | collective-permute-start | bytes 1572872 | tf_op jit(solution)/shard_map/ppermute | solution.py:29
  117.0 0.3 fusion
  117.3 5.5 %collective-permute-start.4 = (bf16[8,128,256]{2,1,0:T(8,128)(2,1)S(1)}, bf16[8,128,256]{2,1,0:T(8,128)(2,1)S(1)}, u32[]{:S(2)}, u32[]{:S(2)}) collective-permute-start(bf16[8,128,256]{2,1,0:T(8,128)(2,1)S(1)} %fusion), channel_id=1, source_target_pairs={{0,2},{2,4},{4,6},{6,8},{8,10},{10,12},{12,14},{14,16},{16,18},{18... | collective-permute-start | bytes 1572872 | tf_op jit(solution)/shard_map/ppermute | solution.py:29
  122.9 2.6 %collective-permute-done.8 = bf16[8,128,256]{2,1,0:T(8,128)(2,1)S(1)} collective-permute-done((bf16[8,128,256]{2,1,0:T(8,128)(2,1)S(1)}, bf16[8,128,256]{2,1,0:T(8,128)(2,1)S(1)}, u32[]{:S(2)}, u32[]{:S(2)}) %collective-permute-start.8) | collective-permute-done | bytes 524320 | tf_op jit(solution)/shard_map/ppermute | solution.py:29
  125.5 0.3 fusion.1
  125.8 5.2 %collective-permute-start.9 = (bf16[8,128,256]{2,1,0:T(8,128)(2,1)S(1)}, bf16[8,128,256]{2,1,0:T(8,128)(2,1)S(1)}, u32[]{:S(2)}, u32[]{:S(2)}) collective-permute-start(bf16[8,128,256]{2,1,0:T(8,128)(2,1)S(1)} %fusion.1), channel_id=1, source_target_pairs={{0,2},{2,4},{4,6},{6,8},{8,10},{10,12},{12,14},{14,16},{16,18},{18... | collective-permute-start | bytes 1572872 | tf_op jit(solution)/shard_map/ppermute | solution.py:29
  131.0 0.7 collective-permute-start.5
  131.8 0.9 collective-permute-start.10
  132.7 17.8 %collective-permute-done.4 = bf16[8,128,256]{2,1,0:T(8,128)(2,1)S(1)} collective-permute-done((bf16[8,128,256]{2,1,0:T(8,128)(2,1)S(1)}, bf16[8,128,256]{2,1,0:T(8,128)(2,1)S(1)}, u32[]{:S(2)}, u32[]{:S(2)}) %collective-permute-start.4) | collective-permute-done | bytes 524320 | tf_op jit(solution)/shard_map/ppermute | solution.py:29
  150.5 0.9 fusion.2.refs_2_
  151.4 0.0 collective-permute-done.10
  151.4 10.4 %collective-permute-done.9 = bf16[8,128,256]{2,1,0:T(8,128)(2,1)S(1)} collective-permute-done((bf16[8,128,256]{2,1,0:T(8,128)(2,1)S(1)}, bf16[8,128,256]{2,1,0:T(8,128)(2,1)S(1)}, u32[]{:S(2)}, u32[]{:S(2)}) %collective-permute-start.9) | collective-permute-done | bytes 524320 | tf_op jit(solution)/shard_map/ppermute | solution.py:29
  161.9 0.9 fusion.3.refs_3_
  162.8 13.0 %shard_map.112 = bf16[512,2048]{1,0:T(8,128)(2,1)} custom-call(s32[1]{0:T(128)} %bitcast.20.first_ref, bf16[8,1024,256]{2,1,0:T(8,128)(2,1)} %get-tuple-element.9.refs_0_, bf16[8,1024,256]{2,1,0:T(8,128)(2,1)} %get-tuple-element.10.refs_1_, bf16[8,128,128]{2,1,0:T(8,128)(2,1)} %fusion.2.refs_2_, bf16[8,128,128]{2,1,0:T(8,128)(2,1)} %fusion.3.refs_3_, ...), custom_call_target="tpu_custom_call" | custom-call | flops 4294967296 | bytes 25165824 | tf_op jit(solution)/shard_map/pallas_call | solution.py:283
  175.8 13.3 %collective-permute-start.11 = (bf16[512,2048]{1,0:T(8,128)(2,1)}, bf16[512,2048]{1,0:T(8,128)(2,1)S(1)}, u32[]{:S(2)}, u32[]{:S(2)}) collective-permute-start(bf16[512,2048]{1,0:T(8,128)(2,1)} %shard_map.112), channel_id=1, source_target_pairs={{0,1},{1,0},{2,3},{3,2},{4,5},{5,4},{6,7},{7,6},{8,9},{9,8},{10,11... | collective-permute-start | bytes 6291464 | tf_op jit(solution)/shard_map/ppermute | solution.py:377
  189.1 13.1 %shard_map.111 = bf16[512,2048]{1,0:T(8,128)(2,1)} custom-call(s32[1]{0:T(128)} %bitcast.first_ref, bf16[8,1024,256]{2,1,0:T(8,128)(2,1)} %get-tuple-element.9.refs_0_, bf16[8,1024,256]{2,1,0:T(8,128)(2,1)} %get-tuple-element.10.refs_1_, bf16[8,128,128]{2,1,0:T(8,128)(2,1)} %fusion.2.refs_2_, bf16[8,128,128]{2,1,0:T(8,128)(2,1)} %fusion.3.refs_3_, ...), custom_call_target="tpu_custom_call" | custom-call | flops 4294967296 | bytes 25165824 | tf_op jit(solution)/shard_map/pallas_call | solution.py:283
  202.1 4.4 %convert_add_fusion = f32[512,2048]{1,0:T(8,128)} fusion(bf16[512,2048]{1,0:T(8,128)(2,1)S(1)} %collective-permute-done.11, bf16[512,2048]{1,0:T(8,128)(2,1)} %shard_map.111), kind=kLoop, calls=%fused_computation | loop fusion | flops 3145728 | bytes 8388608 | tf_op jit(solution)/shard_map/add | solution.py:379
  (20 shorter events, 0.3 us)
Async XLA Ops:
  0.0 5.3 %copy-start = (f32[16,1024]{1,0:T(8,128)S(1)}, f32[16,1024]{1,0:T(8,128)}, u32[]{:S(2)}) copy-start(f32[16,1024]{1,0:T(8,128)} %param.15) | copy-start | bytes 196612
  2.2 8.9 %collective-permute-start = (f32[3,32,128]{2,1,0:T(8,128)S(1)}, f32[3,32,128]{2,1,0:T(8,128)S(1)}, u32[]{:S(2)}, u32[]{:S(2)}) collective-permute-start(f32[3,32,128]{2,1,0:T(8,128)S(1)} %pad_maximum_fusion), channel_id=1, source_target_pairs={{0,2},{2,4},{4,6},{6,8},{8,10},{10,12},{12,14},{14,16},{16,18},{18... | collective-permute-start | bytes 147464 | tf_op jit(solution)/shard_map/ppermute | solution.py:29
  42.2 37.4 %collective-permute-start.1 = (bf16[8,128,256]{2,1,0:T(8,128)(2,1)S(1)}, bf16[8,128,256]{2,1,0:T(8,128)(2,1)S(1)}, u32[]{:S(2)}, u32[]{:S(2)}) collective-permute-start(bf16[8,128,256]{2,1,0:T(8,128)(2,1)S(1)} %convert.18), channel_id=1, source_target_pairs={{0,2},{2,4},{4,6},{6,8},{8,10},{10,12},{12,14},{14,16},{16,18},{18... | collective-permute-start | bytes 1572872 | tf_op jit(solution)/shard_map/ppermute | solution.py:29
  45.3 33.1 %copy-start.2 = (f32[8,128,256]{2,1,0:T(8,128)S(1)}, f32[8,128,256]{2,1,0:T(8,128)}, u32[]{:S(2)}) copy-start(f32[8,128,256]{2,1,0:T(8,128)} %get-tuple-element.11) | copy-start | bytes 3145732
  75.3 20.4 %collective-permute-start.6 = (bf16[8,128,256]{2,1,0:T(8,128)(2,1)S(1)}, bf16[8,128,256]{2,1,0:T(8,128)(2,1)S(1)}, u32[]{:S(2)}, u32[]{:S(2)}) collective-permute-start(bf16[8,128,256]{2,1,0:T(8,128)(2,1)S(1)} %convert.21), channel_id=1, source_target_pairs={{0,2},{2,4},{4,6},{6,8},{8,10},{10,12},{12,14},{14,16},{16,18},{18... | collective-permute-start | bytes 1572872 | tf_op jit(solution)/shard_map/ppermute | solution.py:29
  79.8 22.7 %collective-permute-start.2 = (bf16[8,128,256]{2,1,0:T(8,128)(2,1)S(1)}, bf16[8,128,256]{2,1,0:T(8,128)(2,1)S(1)}, u32[]{:S(2)}, u32[]{:S(2)}) collective-permute-start(bf16[8,128,256]{2,1,0:T(8,128)(2,1)S(1)} %get-tuple-element.19), channel_id=1, source_target_pairs={{0,4},{2,6},{4,8},{6,10},{8,12},{10,14},{12,16},{14,18},{16,20},{1... | collective-permute-start | bytes 1572872 | tf_op jit(solution)/shard_map/ppermute | solution.py:29
  96.0 17.4 %collective-permute-start.7 = (bf16[8,128,256]{2,1,0:T(8,128)(2,1)S(1)}, bf16[8,128,256]{2,1,0:T(8,128)(2,1)S(1)}, u32[]{:S(2)}, u32[]{:S(2)}) collective-permute-start(bf16[8,128,256]{2,1,0:T(8,128)(2,1)S(1)} %get-tuple-element.23), channel_id=1, source_target_pairs={{0,4},{2,6},{4,8},{6,10},{8,12},{10,14},{12,16},{14,18},{16,20},{1... | collective-permute-start | bytes 1572872 | tf_op jit(solution)/shard_map/ppermute | solution.py:29
  102.8 14.2 %collective-permute-start.3 = (bf16[8,128,256]{2,1,0:T(8,128)(2,1)S(1)}, bf16[8,128,256]{2,1,0:T(8,128)(2,1)S(1)}, u32[]{:S(2)}, u32[]{:S(2)}) collective-permute-start(bf16[8,128,256]{2,1,0:T(8,128)(2,1)S(1)} %get-tuple-element.21), channel_id=1, source_target_pairs={{0,8},{2,10},{4,12},{6,14},{8,16},{10,18},{12,20},{14,22},{16,24},... | collective-permute-start | bytes 1572872 | tf_op jit(solution)/shard_map/ppermute | solution.py:29
  113.7 11.8 %collective-permute-start.8 = (bf16[8,128,256]{2,1,0:T(8,128)(2,1)S(1)}, bf16[8,128,256]{2,1,0:T(8,128)(2,1)S(1)}, u32[]{:S(2)}, u32[]{:S(2)}) collective-permute-start(bf16[8,128,256]{2,1,0:T(8,128)(2,1)S(1)} %get-tuple-element.25), channel_id=1, source_target_pairs={{0,8},{2,10},{4,12},{6,14},{8,16},{10,18},{12,20},{14,22},{16,24},... | collective-permute-start | bytes 1572872 | tf_op jit(solution)/shard_map/ppermute | solution.py:29
  117.3 33.2 %collective-permute-start.4 = (bf16[8,128,256]{2,1,0:T(8,128)(2,1)S(1)}, bf16[8,128,256]{2,1,0:T(8,128)(2,1)S(1)}, u32[]{:S(2)}, u32[]{:S(2)}) collective-permute-start(bf16[8,128,256]{2,1,0:T(8,128)(2,1)S(1)} %fusion), channel_id=1, source_target_pairs={{0,2},{2,4},{4,6},{6,8},{8,10},{10,12},{12,14},{14,16},{16,18},{18... | collective-permute-start | bytes 1572872 | tf_op jit(solution)/shard_map/ppermute | solution.py:29
  125.8 36.1 %collective-permute-start.9 = (bf16[8,128,256]{2,1,0:T(8,128)(2,1)S(1)}, bf16[8,128,256]{2,1,0:T(8,128)(2,1)S(1)}, u32[]{:S(2)}, u32[]{:S(2)}) collective-permute-start(bf16[8,128,256]{2,1,0:T(8,128)(2,1)S(1)} %fusion.1), channel_id=1, source_target_pairs={{0,2},{2,4},{4,6},{6,8},{8,10},{10,12},{12,14},{14,16},{16,18},{18... | collective-permute-start | bytes 1572872 | tf_op jit(solution)/shard_map/ppermute | solution.py:29
  131.0 1.6 collective-permute-start.5
  131.8 19.7 %collective-permute-start.10 = (bf16[8,128,128]{2,1,0:T(8,128)(2,1)S(1)}, bf16[8,128,128]{2,1,0:T(8,128)(2,1)S(1)}, u32[]{:S(2)}, u32[]{:S(2)}) collective-permute-start(bf16[8,128,128]{2,1,0:T(8,128)(2,1)S(1)} %slice.142), channel_id=1, source_target_pairs={{0,18},{2,20},{4,22},{6,24},{8,26},{10,28},{12,30},{1,19},{3,21},{... | collective-permute-start | bytes 786440 | tf_op jit(solution)/shard_map/ppermute | solution.py:29
  175.8 26.3 %collective-permute-start.11 = (bf16[512,2048]{1,0:T(8,128)(2,1)}, bf16[512,2048]{1,0:T(8,128)(2,1)S(1)}, u32[]{:S(2)}, u32[]{:S(2)}) collective-permute-start(bf16[512,2048]{1,0:T(8,128)(2,1)} %shard_map.112), channel_id=1, source_target_pairs={{0,1},{1,0},{2,3},{3,2},{4,5},{5,4},{6,7},{7,6},{8,9},{9,8},{10,11... | collective-permute-start | bytes 6291464 | tf_op jit(solution)/shard_map/ppermute | solution.py:377
  189.1 17.4 %copy-start.1 = (f32[16,1024]{1,0:T(8,128)S(1)}, f32[16,1024]{1,0:T(8,128)}, u32[]{:S(2)}) copy-start(f32[16,1024]{1,0:T(8,128)} %param.15) | copy-start | bytes 196612

commit v3 on v2

--- a/solution.py
+++ b/solution.py
@@ -56,8 +56,7 @@
     k_w,
     v_w,
     crow_ref,
-    ccol_ref,
-    bcol_ref,
+    brow_ref,
     out_ref,
     fin_ref,
     state,
@@ -91,7 +90,9 @@
         return (row // size) == (col // size)
 
     count = kgroup * ratio
-    keys, keys_t, lifted, scores, mixing, rhs = [], [], [], [], [], []
+    ccol = crow_ref[...].T
+    bcol = brow_ref[...].T
+    keys_t, lifted, scores, mixing, rhs = [], [], [], [], []
     for i in range(kgroup):
         q = unit_rows(conv_head(q_ref, q_old, q_w, kfirst + i, kheads, chunk, taps), width**-0.5)
         k = unit_rows(conv_head(k_ref, k_old, k_w, kfirst + i, kheads, chunk, taps))
@@ -101,8 +102,8 @@
         for r in range(ratio):
             v = i * ratio + r
             values = conv_head(v_ref, v_old, v_w, kfirst * ratio + v, vheads, chunk, taps)
-            cc = ccol_ref[:, v : v + 1]
-            b = bcol_ref[:, v : v + 1]
+            cc = ccol[:, v : v + 1]
+            b = bcol[:, v : v + 1]
             decay = jnp.exp(jnp.minimum(cc - crow_ref[v : v + 1, :], 0.0))
             lift = jnp.exp(cc)
             mixing.append(jnp.where(strict, -(b * inner * decay), 0.0))
@@ -151,7 +152,7 @@
         right = jnp.concatenate([narrow[v], update[v].astype(jnp.bfloat16)], axis=0)
         out_ref[v] = mm(left, right).astype(out_ref.dtype)
         last = crow_ref[v : v + 1, chunk - 1 : chunk]
-        fade = jnp.exp(last - ccol_ref[:, v : v + 1])
+        fade = jnp.exp(last - ccol[:, v : v + 1])
         state[v] = jnp.exp(last) * states[v] + mm(keys_t[v], fade * update[v])
 
     for old, ref, heads in ((q_old, q_ref, kheads), (k_old, k_ref, kheads), (v_old, v_ref, vheads)):
@@ -188,8 +189,7 @@
             whole(taps * kheads),
             whole(taps * vheads),
             pl.BlockSpec((count, chunk), lambda c: (group, c)),
-            pl.BlockSpec((chunk, count), lambda c: (c, 0)),
-            pl.BlockSpec((chunk, count), lambda c: (c, 0)),
+            pl.BlockSpec((count, chunk), lambda c: (group, c)),
         ],
         out_specs=[
             pl.BlockSpec((count, chunk, 2 * width), lambda c: (0, c, 0)),
@@ -214,40 +214,102 @@
     )(*arrays)
 
 
-def enter_state(final):
-    width = final.shape[1]
-
-    def compose(later, earlier):
-        return jnp.einsum(
-            "hij,hjk->hik",
-            later[:, :, :width].astype(jnp.bfloat16),
-            earlier,
-            preferred_element_type=jnp.float32,
+def chain_kernel(groups, *refs):
+    finals, enter_ref = refs[:groups], refs[groups]
+    arrived, leaving, send_sem, recv_sem = refs[groups + 1 :]
+    n = lax.axis_size("ctx")
+    me = lax.axis_index("ctx")
+    right, left = lax.rem(me + 1, n), lax.rem(me + n - 1, n)
+    count, width = finals[0].shape[0], finals[0].shape[1]
+
+    barrier = pltpu.get_barrier_semaphore()
+    for neighbour in (left, right):
+        pl.semaphore_signal(
+            barrier, inc=1, device_id={"ctx": neighbour}, device_id_type=pl.DeviceIdType.MESH
         )
-
-    count = lax.axis_size("ctx")
-    empty = jnp.zeros((final.shape[0], width, width), jnp.float32)
-    pair, reach = final, 1
-    while 2 * reach < count:
-        earlier = from_behind(pair.astype(jnp.bfloat16), "ctx", reach)
-        pair = compose(pair, earlier) + jnp.concatenate([empty, pair[:, :, width:]], axis=2)
-        reach *= 2
-    sent = pair.astype(jnp.bfloat16)
-    near = from_behind(sent, "ctx", 1)
-    far = from_behind(sent[:, :, width:], "ctx", reach + 1)
-    return (compose(near, far) + near[:, :, width:].astype(jnp.float32)).astype(jnp.bfloat16)
+    pl.semaphore_wait(barrier, 2)
+
+    def hop(head):
+        return pltpu.make_async_remote_copy(
+            src_ref=leaving.at[head],
+            dst_ref=arrived.at[head],
+            send_sem=send_sem.at[head],
+            recv_sem=recv_sem.at[head],
+            device_id={"ctx": right},
+            device_id_type=pl.DeviceIdType.MESH,
+        )
+
+    for g in range(groups):
+        final = finals[g]
+
+        def turn(v, carry, final=final, g=g):
+            head = g * count + v
+
+            @pl.when(me == 0)
+            def _():
+                enter_ref[head] = jnp.zeros((width, width), jnp.bfloat16)
+                leaving[head] = final[v, :, width:].astype(jnp.bfloat16)
+
+            @pl.when(me > 0)
+            def _():
+                hop(head).wait_recv()
+                received = arrived[head]
+                enter_ref[head] = received
+                leaving[head] = (
+                    mm(final[v, :, :width], received) + final[v, :, width:]
+                ).astype(jnp.bfloat16)
+
+            @pl.when(me < n - 1)
+            def _():
+                hop(head).start()
+
+            return carry
+
+        lax.fori_loop(0, count, turn, 0)
+
+    @pl.when(me < n - 1)
+    def _():
+        def settle(head, carry):
+            hop(head).wait_send()
+            return carry
+
+        lax.fori_loop(0, groups * count, settle, 0)
+
+
+def enter_states(finals):
+    groups = len(finals)
+    count, width, _ = finals[0].shape
+    heads = groups * count
+    return pl.pallas_call(
+        functools.partial(chain_kernel, groups),
+        out_shape=jax.ShapeDtypeStruct((heads, width, width), jnp.bfloat16),
+        in_specs=[pl.BlockSpec(memory_space=pltpu.VMEM)] * groups,
+        out_specs=pl.BlockSpec(memory_space=pltpu.VMEM),
+        scratch_shapes=[
+            pltpu.VMEM((heads, width, width), jnp.bfloat16),
+            pltpu.VMEM((heads, width, width), jnp.bfloat16),
+            pltpu.SemaphoreType.DMA((heads,)),
+            pltpu.SemaphoreType.DMA((heads,)),
+        ],
+        compiler_params=pltpu.CompilerParams(
+            collective_id=0, has_side_effects=True, vmem_limit_bytes=VMEM_LIMIT
+        ),
+        cost_estimate=pl.CostEstimate(
+            flops=2 * heads * width**3, bytes_accessed=12 * heads * width**2, transcendentals=0
+        ),
+    )(*finals)
 
 
 def mix_kernel(groups, rows, vheads, first_ref, *refs):
-    outs, enters = refs[:groups], refs[groups : 2 * groups]
-    gate_ref, gain_ref, weight_ref, part_ref, normed = refs[2 * groups :]
+    outs = refs[:groups]
+    enter_ref, gate_ref, gain_ref, weight_ref, part_ref, normed = refs[groups:]
     width = gain_ref.shape[1]
     count = vheads // groups
     for g in range(groups):
         for v in range(count):
             head = g * count + v
             own = outs[g][v]
-            recurrent = own[:, width:].astype(jnp.float32) + mm(own[:, :width], enters[g][v])
+            recurrent = own[:, width:].astype(jnp.float32) + mm(own[:, :width], enter_ref[head])
             mean = jnp.sum(recurrent * recurrent, axis=-1, keepdims=True) * (1.0 / width)
             gate = gate_ref[pl.ds(head, rows, stride=vheads), :]
             scaled = recurrent * lax.rsqrt(mean + norm_epsilon) * gain_ref[...] * silu(gate)
@@ -271,8 +333,8 @@
         num_scalar_prefetch=1,
         grid=(tokens // rows,),
         in_specs=[pl.BlockSpec((count, rows, double), lambda t, s: (0, s[0] + t, 0))] * groups
-        + [pl.BlockSpec((count, width, width), lambda t, s: (0, 0, 0))] * groups
         + [
+            pl.BlockSpec((vheads, width, width), lambda t, s: (0, 0, 0)),
             pl.BlockSpec((rows * vheads, width), lambda t, s: (s[0] + t, 0)),
             pl.BlockSpec((1, width), lambda t, s: (0, 0)),
             pl.BlockSpec((depth, columns), lambda t, s: (0, 0)),
@@ -292,7 +354,7 @@
             bytes_accessed=2 * depth * columns + 16 * tokens * depth,
             transcendentals=tokens * depth,
         ),
-    )((first // rows).astype(jnp.int32).reshape(1), *outs, *enters, gate, gain, weight)
+    )((first // rows).astype(jnp.int32).reshape(1), *outs, enters, gate, gain, weight)
 
 
 def on_device(
@@ -335,9 +397,8 @@
     ).reshape(vheads, tokens)
 
     kgroup = min(4, kheads)
-    outs, enters = [], []
+    outs, finals = [], []
     for kfirst in range(0, kheads, kgroup):
-        picked = slice(kfirst * ratio, (kfirst + kgroup) * ratio)
         out, final = chunk_call(
             (chunk, kheads, vheads, kfirst, kgroup, taps),
             tokens,
@@ -353,12 +414,12 @@
                 flat(key_conv),
                 flat(value_conv),
                 summed,
-                summed[picked].T,
-                strength[picked].T,
+                strength,
             ),
         )
         outs.append(out)
-        enters.append(enter_state(final))
+        finals.append(final)
+    enters = enter_states(finals)
 
     shares = lax.axis_size("head")
     gate = flat(gate_in)

time: 207 us -> 162 us (0.78)
  the two profiles are of different devices: /device:TPU:17 before, /device:TPU:31 now
where the time goes in v3:
time: 162 us
  Pallas kernels  137 us (85%)
  starting transfers between devices  13.6 us (8%)
  other arithmetic  4.37 us (3%)
  local copies, waits for them, and re-layouts  4.07 us (3%)
  waiting for transfers between devices  2.59 us (2%)
    pallas_call x2, Pallas kernels, chunk_call(): pl.pallas_call(functools.partial(chunk_kernel, meta), grid=(tokens // chu...  57.1 us
    pallas_call x1, Pallas kernels, enter_states(): pl.pallas_call(functools.partial(chain_kernel, groups), out_shape=jax.Sha...  53.8 us
    pallas_call x2, Pallas kernels, mix_call(): pl.pallas_call(functools.partial(mix_kernel, groups, rows, vheads), grid_...  25.8 us
    ppermute x1, starting transfers between devices, on_device(): arrived = lax.ppermute(other, 'head', [(0, 1), (1, 0)])  12.3 us
    add x1, other arithmetic, on_device(): return own.astype(jnp.float32) + arrived.astype(jnp.float32)  4.36 us
  transfers between devices with their start and end apart: 2, of which 1 were waited for; matrix products, arithmetic and copies ran while one was open for 1% of the time, Pallas kernels for 8%

profile of v3, /device:TPU:31, one launch (start us, length us, event | category | flops | bytes accessed | tf_op | source)
XLA Modules:
  0.0 161.6 jit_solution(8181980270058550508)
XLA Ops:
  0.0 0.0 copy-start
  0.0 0.7 slice.18
  0.7 0.7 slice.19
  1.5 0.7 slice.20
  2.2 1.3 collective-permute-start
  3.5 0.0 copy-done
  3.5 0.3 convolution_bitcast_fusion
  3.8 0.6 copy.21
  4.4 2.6 %collective-permute-done = f32[3,32,128]{2,1,0:T(8,128)S(1)} collective-permute-done((f32[3,32,128]{2,1,0:T(8,128)S(1)}, f32[3,32,128]{2,1,0:T(8,128)S(1)}, u32[]{:S(2)}, u32[]{:S(2)}) %collective-permute-start) | collective-permute-done | bytes 49184 | tf_op jit(solution)/shard_map/ppermute | solution.py:29
  7.0 0.6 pad_slice_fusion
  7.6 0.6 fusion.5
  8.3 28.6 %shard_map.110 = (bf16[8,1024,256]{2,1,0:T(8,128)(2,1)}, f32[8,128,256]{2,1,0:T(8,128)}) custom-call(f32[8192,128]{1,0:T(8,128)} %bitcast.41, f32[8192,128]{1,0:T(8,128)} %bitcast.43, f32[16384,128]{1,0:T(8,128)} %bitcast.39, f32[64,128]{1,0:T(8,128)} %get-tuple-element.14.q_rim, f32[64,128]{1,0:T(8,128)} %get-tuple-element.13.k_rim, f32[128,128]{1,0:T(8,128)} %bitcast.33, ...), custom_call_target="tpu_custom_call" | custom-call | flops 5368709120 | bytes 25165824 | tf_op jit(solution)/shard_map/pallas_call | solution.py:178
  36.9 28.5 %shard_map.109 = (bf16[8,1024,256]{2,1,0:T(8,128)(2,1)}, f32[8,128,256]{2,1,0:T(8,128)}) custom-call(f32[8192,128]{1,0:T(8,128)} %bitcast.42, f32[8192,128]{1,0:T(8,128)} %bitcast.44, f32[16384,128]{1,0:T(8,128)} %bitcast.40, f32[64,128]{1,0:T(8,128)} %get-tuple-element.14.q_rim, f32[64,128]{1,0:T(8,128)} %get-tuple-element.13.k_rim, f32[128,128]{1,0:T(8,128)} %bitcast.34, ...), custom_call_target="tpu_custom_call" | custom-call | flops 5368709120 | bytes 25165824 | tf_op jit(solution)/shard_map/pallas_call | solution.py:178
  65.4 53.8 %shard_map.111.refs_2_ = bf16[16,128,128]{2,1,0:T(8,128)(2,1)} custom-call(f32[8,128,256]{2,1,0:T(8,128)} %get-tuple-element.11.refs_0_, f32[8,128,256]{2,1,0:T(8,128)} %get-tuple-element.12.refs_1_), custom_call_target="tpu_custom_call" | custom-call | flops 67108864 | bytes 3145728 | tf_op jit(solution)/shard_map/pallas_call | solution.py:283
  119.2 12.9 %shard_map.113 = bf16[512,2048]{1,0:T(8,128)(2,1)} custom-call(s32[1]{0:T(128)} %bitcast.14.first_ref, bf16[8,1024,256]{2,1,0:T(8,128)(2,1)} %get-tuple-element.9.refs_0_, bf16[8,1024,256]{2,1,0:T(8,128)(2,1)} %get-tuple-element.10.refs_1_, bf16[16,128,128]{2,1,0:T(8,128)(2,1)} %shard_map.111.refs_2_, f32[16384,128]{1,0:T(8,128)} %bitcast.31, ...), custom_call_target="tpu_custom_call" | custom-call | flops 4294967296 | bytes 25165824 | tf_op jit(solution)/shard_map/pallas_call | solution.py:345
  132.1 12.3 %collective-permute-start.1 = (bf16[512,2048]{1,0:T(8,128)(2,1)}, bf16[512,2048]{1,0:T(8,128)(2,1)S(1)}, u32[]{:S(2)}, u32[]{:S(2)}) collective-permute-start(bf16[512,2048]{1,0:T(8,128)(2,1)} %shard_map.113), channel_id=1, source_target_pairs={{0,1},{1,0},{2,3},{3,2},{4,5},{5,4},{6,7},{7,6},{8,9},{9,8},{10,11... | collective-permute-start | bytes 6291464 | tf_op jit(solution)/shard_map/ppermute | solution.py:438
  144.4 12.9 %shard_map.112 = bf16[512,2048]{1,0:T(8,128)(2,1)} custom-call(s32[1]{0:T(128)} %bitcast.first_ref, bf16[8,1024,256]{2,1,0:T(8,128)(2,1)} %get-tuple-element.9.refs_0_, bf16[8,1024,256]{2,1,0:T(8,128)(2,1)} %get-tuple-element.10.refs_1_, bf16[16,128,128]{2,1,0:T(8,128)(2,1)} %shard_map.111.refs_2_, f32[16384,128]{1,0:T(8,128)} %bitcast.32, ...), custom_call_target="tpu_custom_call" | custom-call | flops 4294967296 | bytes 25165824 | tf_op jit(solution)/shard_map/pallas_call | solution.py:345
  157.2 0.0 collective-permute-done.1
  157.2 4.4 %convert_add_fusion = f32[512,2048]{1,0:T(8,128)} fusion(bf16[512,2048]{1,0:T(8,128)(2,1)S(1)} %collective-permute-done.1, bf16[512,2048]{1,0:T(8,128)(2,1)} %shard_map.112), kind=kLoop, calls=%fused_computation | loop fusion | flops 3145728 | bytes 8388608 | tf_op jit(solution)/shard_map/add | solution.py:440
  (2 shorter events, 0.0 us)
Async XLA Ops:
  0.0 3.5 %copy-start = (f32[16,1024]{1,0:T(8,128)S(1)}, f32[16,1024]{1,0:T(8,128)}, u32[]{:S(2)}) copy-start(f32[16,1024]{1,0:T(8,128)} %param.15) | copy-start | bytes 196612
  2.2 4.8 %collective-permute-start = (f32[3,32,128]{2,1,0:T(8,128)S(1)}, f32[3,32,128]{2,1,0:T(8,128)S(1)}, u32[]{:S(2)}, u32[]{:S(2)}) collective-permute-start(f32[3,32,128]{2,1,0:T(8,128)S(1)} %pad_maximum_fusion), channel_id=1, source_target_pairs={{0,2},{2,4},{4,6},{6,8},{8,10},{10,12},{12,14},{14,16},{16,18},{18... | collective-permute-start | bytes 147464 | tf_op jit(solution)/shard_map/ppermute | solution.py:29
  132.1 25.2 %collective-permute-start.1 = (bf16[512,2048]{1,0:T(8,128)(2,1)}, bf16[512,2048]{1,0:T(8,128)(2,1)S(1)}, u32[]{:S(2)}, u32[]{:S(2)}) collective-permute-start(bf16[512,2048]{1,0:T(8,128)(2,1)} %shard_map.113), channel_id=1, source_target_pairs={{0,1},{1,0},{2,3},{3,2},{4,5},{5,4},{6,7},{7,6},{8,9},{9,8},{10,11... | collective-permute-start | bytes 6291464 | tf_op jit(solution)/shard_map/ppermute | solution.py:438

commit v4 on v3

--- a/solution.py
+++ b/solution.py
@@ -245,24 +245,24 @@
         def turn(v, carry, final=final, g=g):
             head = g * count + v
 
+            through = final[v, :, :width].astype(jnp.bfloat16)
+            offset = final[v, :, width:]
+
             @pl.when(me == 0)
             def _():
-                enter_ref[head] = jnp.zeros((width, width), jnp.bfloat16)
-                leaving[head] = final[v, :, width:].astype(jnp.bfloat16)
+                leaving[head] = offset.astype(jnp.bfloat16)
+                arrived[head] = jnp.zeros((width, width), jnp.bfloat16)
 
             @pl.when(me > 0)
             def _():
                 hop(head).wait_recv()
-                received = arrived[head]
-                enter_ref[head] = received
-                leaving[head] = (
-                    mm(final[v, :, :width], received) + final[v, :, width:]
-                ).astype(jnp.bfloat16)
+                leaving[head] = (mm(through, arrived[head]) + offset).astype(jnp.bfloat16)
 
             @pl.when(me < n - 1)
             def _():
                 hop(head).start()
 
+            enter_ref[head] = arrived[head]
             return carry
 
         lax.fori_loop(0, count, turn, 0)

time: 162 us -> 162 us (level)
  no operation moved by 1% of the time
where the time goes in v4:
time: 162 us
  Pallas kernels  137 us (85%)
  starting transfers between devices  13.6 us (8%)
  other arithmetic  4.37 us (3%)
  local copies, waits for them, and re-layouts  4.07 us (3%)
  waiting for transfers between devices  2.59 us (2%)
    pallas_call x2, Pallas kernels, chunk_call(): pl.pallas_call(functools.partial(chunk_kernel, meta), grid=(tokens // chu...  57.1 us
    pallas_call x1, Pallas kernels, enter_states(): pl.pallas_call(functools.partial(chain_kernel, groups), out_shape=jax.Sha...  53.9 us
    pallas_call x2, Pallas kernels, mix_call(): pl.pallas_call(functools.partial(mix_kernel, groups, rows, vheads), grid_...  25.8 us
    ppermute x1, starting transfers between devices, on_device(): arrived = lax.ppermute(other, 'head', [(0, 1), (1, 0)])  12.3 us
    add x1, other arithmetic, on_device(): return own.astype(jnp.float32) + arrived.astype(jnp.float32)  4.36 us
  transfers between devices with their start and end apart: 2, of which 1 were waited for; matrix products, arithmetic and copies ran while one was open for 1% of the time, Pallas kernels for 8%

profile of v4, /device:TPU:31, one launch (start us, length us, event | category | flops | bytes accessed | tf_op | source)
XLA Modules:
  0.0 161.7 jit_solution(17772074065222559366)
XLA Ops:
  0.0 0.0 copy-start
  0.0 0.7 slice.18
  0.7 0.7 slice.19
  1.5 0.7 slice.20
  2.2 1.3 collective-permute-start
  3.5 0.0 copy-done
  3.5 0.3 convolution_bitcast_fusion
  3.8 0.6 copy.21
  4.4 2.6 %collective-permute-done = f32[3,32,128]{2,1,0:T(8,128)S(1)} collective-permute-done((f32[3,32,128]{2,1,0:T(8,128)S(1)}, f32[3,32,128]{2,1,0:T(8,128)S(1)}, u32[]{:S(2)}, u32[]{:S(2)}) %collective-permute-start) | collective-permute-done | bytes 49184 | tf_op jit(solution)/shard_map/ppermute | solution.py:29
  7.0 0.6 pad_slice_fusion
  7.6 0.6 fusion.5
  8.3 28.6 %shard_map.110 = (bf16[8,1024,256]{2,1,0:T(8,128)(2,1)}, f32[8,128,256]{2,1,0:T(8,128)}) custom-call(f32[8192,128]{1,0:T(8,128)} %bitcast.41, f32[8192,128]{1,0:T(8,128)} %bitcast.43, f32[16384,128]{1,0:T(8,128)} %bitcast.39, f32[64,128]{1,0:T(8,128)} %get-tuple-element.14.q_rim, f32[64,128]{1,0:T(8,128)} %get-tuple-element.13.k_rim, f32[128,128]{1,0:T(8,128)} %bitcast.33, ...), custom_call_target="tpu_custom_call" | custom-call | flops 5368709120 | bytes 25165824 | tf_op jit(solution)/shard_map/pallas_call | solution.py:178
  36.9 28.5 %shard_map.109 = (bf16[8,1024,256]{2,1,0:T(8,128)(2,1)}, f32[8,128,256]{2,1,0:T(8,128)}) custom-call(f32[8192,128]{1,0:T(8,128)} %bitcast.42, f32[8192,128]{1,0:T(8,128)} %bitcast.44, f32[16384,128]{1,0:T(8,128)} %bitcast.40, f32[64,128]{1,0:T(8,128)} %get-tuple-element.14.q_rim, f32[64,128]{1,0:T(8,128)} %get-tuple-element.13.k_rim, f32[128,128]{1,0:T(8,128)} %bitcast.34, ...), custom_call_target="tpu_custom_call" | custom-call | flops 5368709120 | bytes 25165824 | tf_op jit(solution)/shard_map/pallas_call | solution.py:178
  65.4 53.9 %shard_map.111.refs_2_ = bf16[16,128,128]{2,1,0:T(8,128)(2,1)} custom-call(f32[8,128,256]{2,1,0:T(8,128)} %get-tuple-element.11.refs_0_, f32[8,128,256]{2,1,0:T(8,128)} %get-tuple-element.12.refs_1_), custom_call_target="tpu_custom_call" | custom-call | flops 67108864 | bytes 3145728 | tf_op jit(solution)/shard_map/pallas_call | solution.py:283
  119.2 12.9 %shard_map.113 = bf16[512,2048]{1,0:T(8,128)(2,1)} custom-call(s32[1]{0:T(128)} %bitcast.14.first_ref, bf16[8,1024,256]{2,1,0:T(8,128)(2,1)} %get-tuple-element.9.refs_0_, bf16[8,1024,256]{2,1,0:T(8,128)(2,1)} %get-tuple-element.10.refs_1_, bf16[16,128,128]{2,1,0:T(8,128)(2,1)} %shard_map.111.refs_2_, f32[16384,128]{1,0:T(8,128)} %bitcast.31, ...), custom_call_target="tpu_custom_call" | custom-call | flops 4294967296 | bytes 25165824 | tf_op jit(solution)/shard_map/pallas_call | solution.py:345
  132.1 12.3 %collective-permute-start.1 = (bf16[512,2048]{1,0:T(8,128)(2,1)}, bf16[512,2048]{1,0:T(8,128)(2,1)S(1)}, u32[]{:S(2)}, u32[]{:S(2)}) collective-permute-start(bf16[512,2048]{1,0:T(8,128)(2,1)} %shard_map.113), channel_id=1, source_target_pairs={{0,1},{1,0},{2,3},{3,2},{4,5},{5,4},{6,7},{7,6},{8,9},{9,8},{10,11... | collective-permute-start | bytes 6291464 | tf_op jit(solution)/shard_map/ppermute | solution.py:438
  144.5 12.9 %shard_map.112 = bf16[512,2048]{1,0:T(8,128)(2,1)} custom-call(s32[1]{0:T(128)} %bitcast.first_ref, bf16[8,1024,256]{2,1,0:T(8,128)(2,1)} %get-tuple-element.9.refs_0_, bf16[8,1024,256]{2,1,0:T(8,128)(2,1)} %get-tuple-element.10.refs_1_, bf16[16,128,128]{2,1,0:T(8,128)(2,1)} %shard_map.111.refs_2_, f32[16384,128]{1,0:T(8,128)} %bitcast.32, ...), custom_call_target="tpu_custom_call" | custom-call | flops 4294967296 | bytes 25165824 | tf_op jit(solution)/shard_map/pallas_call | solution.py:345
  157.3 0.0 collective-permute-done.1
  157.3 4.4 %convert_add_fusion = f32[512,2048]{1,0:T(8,128)} fusion(bf16[512,2048]{1,0:T(8,128)(2,1)S(1)} %collective-permute-done.1, bf16[512,2048]{1,0:T(8,128)(2,1)} %shard_map.112), kind=kLoop, calls=%fused_computation | loop fusion | flops 3145728 | bytes 8388608 | tf_op jit(solution)/shard_map/add | solution.py:440
  (2 shorter events, 0.0 us)
Async XLA Ops:
  0.0 3.5 %copy-start = (f32[16,1024]{1,0:T(8,128)S(1)}, f32[16,1024]{1,0:T(8,128)}, u32[]{:S(2)}) copy-start(f32[16,1024]{1,0:T(8,128)} %param.15) | copy-start | bytes 196612
  2.2 4.8 %collective-permute-start = (f32[3,32,128]{2,1,0:T(8,128)S(1)}, f32[3,32,128]{2,1,0:T(8,128)S(1)}, u32[]{:S(2)}, u32[]{:S(2)}) collective-permute-start(f32[3,32,128]{2,1,0:T(8,128)S(1)} %pad_maximum_fusion), channel_id=1, source_target_pairs={{0,2},{2,4},{4,6},{6,8},{8,10},{10,12},{12,14},{14,16},{16,18},{18... | collective-permute-start | bytes 147464 | tf_op jit(solution)/shard_map/ppermute | solution.py:29
  132.1 25.2 %collective-permute-start.1 = (bf16[512,2048]{1,0:T(8,128)(2,1)}, bf16[512,2048]{1,0:T(8,128)(2,1)S(1)}, u32[]{:S(2)}, u32[]{:S(2)}) collective-permute-start(bf16[512,2048]{1,0:T(8,128)(2,1)} %shard_map.113), channel_id=1, source_target_pairs={{0,1},{1,0},{2,3},{3,2},{4,5},{5,4},{6,7},{7,6},{8,9},{9,8},{10,11... | collective-permute-start | bytes 6291464 | tf_op jit(solution)/shard_map/ppermute | solution.py:438
